TPU v7x, 32 devices: a whole 2x2x4 slice. The times are simulated.
32 devices in a mesh: groups: 2 (over x), seq: 16 (over z, y, core).
Axes of the slice: x: 2, y: 2, z: 4, core: 2. Of those that a mesh axis runs over, the one named last changes fastest.
Arguments:
- hidden: bfloat16 [768, 3072], P(('groups', 'seq')), parts along dimension 0, may hold values from -4 to 4
- latents: float32 [768, 64], P(('groups', 'seq')), parts along dimension 0, may hold values from -6 to 6
- base_qkv: bfloat16 [3, 768, 1536], P(None, ('groups', 'seq')), parts along dimension 1, may hold values from -8 to 8
- control_qkv: bfloat16 [3, 768, 1536], P(None, ('groups', 'seq')), parts along dimension 1, may hold values from -8 to 8
- step_index: int32 [1], replicated, may hold values from 0 to 49
- w_join: bfloat16 [3072, 3072], P(None, 'seq'), may hold values from -0.109375 to 0.109375
- w_mod: bfloat16 [512, 6144], replicated, may hold values from -0.25 to 0.25
- w_out: bfloat16 [3072, 64], replicated, may hold values from -0.109375 to 0.109375
Outputs:
- hidden_next: bfloat16 [768, 3072], P(('groups', 'seq')), parts along dimension 0
- velocity: float32 [768, 64], P(('groups', 'seq')), parts along dimension 0
- latents_next: float32 [768, 64], P(('groups', 'seq')), parts along dimension 0
There are 2 independent parts, one for each index of `groups`. A program takes and returns all parts, laid end to end along the dimension named above; an argument that names none is the same for every part. Nothing has to cross between parts.
All inputs are finite; a program needn't handle non-finite values.
Results may differ from a plain program's by a relative error of at most 0.0065.
Values may be sent and summed in bfloat16 or wider, within the bound.
A program may use at most 128 MiB of HBM per device.

v0:
```python
import math

import jax
import jax.numpy as jnp
from jax import lax
from jax.sharding import PartitionSpec as P

D = 3072
HD = 64
TEMB = 512
HEADS = 24
STEPS = 50


def time_terms(step_index):
    step_value = step_index[0].astype(jnp.float32)
    level_now = jnp.cos(0.5 * math.pi * step_value / STEPS)
    level_next = jnp.cos(0.5 * math.pi * (step_value + 1.0) / STEPS)
    half_width = TEMB // 2
    frequency = jnp.exp(
        -math.log(10000.0) * jnp.arange(half_width).astype(jnp.float32) / half_width
    )
    angles = 1000.0 * level_now * frequency
    embedding = jnp.concatenate([jnp.cos(angles), jnp.sin(angles)]).astype(jnp.bfloat16)
    return (embedding, level_next - level_now)


def attend(state, queries, shard_rows):
    running_max, running_sum, weighted = state
    count = shard_rows.shape[1]
    keys_block = shard_rows[0].reshape(count, HEADS, HD)
    values_block = shard_rows[1].reshape(count, HEADS, HD)
    scores = jnp.einsum(
        "qhd,khd->qhk", queries, keys_block, preferred_element_type=jnp.float32
    ) * HD ** (-0.5)
    newest_max = jnp.max(scores, axis=2)
    rescale = jnp.exp(running_max - newest_max)
    exponent = jnp.exp(scores - newest_max[:, :, None])
    running_sum = running_sum * rescale + jnp.sum(exponent, axis=2)
    weighted = weighted * rescale[:, :, None] + jnp.einsum(
        "qhk,khd->qhd",
        exponent.astype(jnp.bfloat16),
        values_block,
        preferred_element_type=jnp.float32,
    )
    return (newest_max, running_sum, weighted)


def finish(state):
    running_max, running_sum, weighted = state
    outputs = (weighted / running_sum[:, :, None]).astype(jnp.bfloat16)
    return outputs.reshape(outputs.shape[0], HEADS * HD)


def local(hidden, latents, base_qkv, control_qkv, step_index, w_join, w_mod, w_out):
    tokens_here = hidden.shape[0]
    base_queries = base_qkv[0].reshape(tokens_here, HEADS, HD)
    control_queries = control_qkv[0].reshape(tokens_here, HEADS, HD)
    base_pairs = base_qkv[1:]
    control_pairs = control_qkv[1:]
    initial = (
        jnp.full((tokens_here, HEADS), -jnp.inf, jnp.float32),
        jnp.zeros((tokens_here, HEADS), jnp.float32),
        jnp.zeros((tokens_here, HEADS, HD), jnp.float32),
    )
    base_state = attend(
        initial, base_queries, lax.all_gather(base_pairs, "seq", axis=1, tiled=True)
    )
    control_state = attend(
        initial, control_queries, lax.all_gather(control_pairs, "seq", axis=1, tiled=True)
    )
    joined = jnp.concatenate([finish(base_state), finish(control_state)], axis=1)
    column_part = jnp.dot(
        lax.all_gather(joined, "seq", axis=0, tiled=True),
        w_join,
        preferred_element_type=jnp.float32,
    )
    update = lax.all_to_all(
        column_part.astype(jnp.bfloat16), "seq", split_axis=0, concat_axis=1, tiled=True
    ).astype(column_part.dtype)
    summed = hidden.astype(jnp.float32) + update
    hidden_next = summed.astype(jnp.bfloat16)
    embedding, step_size = time_terms(step_index)
    modulation = jnp.dot(embedding[None, :], w_mod, preferred_element_type=jnp.float32)[0]
    shift_term = modulation[:D]
    gain_term = modulation[D:]
    average = jnp.mean(summed, axis=1, keepdims=True)
    centered = summed - average
    variance = jnp.mean(centered * centered, axis=1, keepdims=True)
    normed = (centered / jnp.sqrt(variance + 1e-05) * (1.0 + gain_term) + shift_term).astype(
        jnp.bfloat16
    )
    velocity = jnp.dot(normed, w_out, preferred_element_type=jnp.float32)
    latents_next = latents + step_size * velocity
    return (hidden_next, velocity, latents_next)


def solution(mesh):
    in_specs = (
        P(("groups", "seq"), None),
        P(("groups", "seq"), None),
        P(None, ("groups", "seq"), None),
        P(None, ("groups", "seq"), None),
        P(),
        P(None, "seq"),
        P(),
        P(),
    )
    out_specs = (P(("groups", "seq"), None), P(("groups", "seq"), None), P(("groups", "seq"), None))
    return jax.shard_map(local, mesh=mesh, in_specs=in_specs, out_specs=out_specs, check_vma=False)
```

profile of v0, /device:TPU:0, one launch (start us, length us, event | category | flops | bytes accessed | tf_op | source)
XLA Modules:
  0.0 176.4 jit_solution(9716021715708989842)
XLA Ops:
  7.2 0.0 copy-start
  7.2 0.0 slice-start.1
  7.2 0.0 slice-start
  7.2 0.0 all-gather.4.cloned.1.call-start
  7.2 1.7 slice.31
  8.9 0.0 all-gather.4.cloned.1.call-update
  8.9 0.0 all-gather.6.cloned.1.call-start
  9.0 1.6 slice.35
  10.6 0.0 all-gather.6.cloned.1.call-update
  10.6 0.0 all-gather.8.cloned.1.call-start
  10.6 0.0 slice-done.1
  10.7 0.8 reshape_squeeze.19
  11.5 0.0 slice-done
  11.5 0.8 reshape_squeeze.22
  12.3 43.0 %all-gather.4.cloned.1.call-done = bf16[2,384,1536]{2,1,0:T(8,128)(2,1)} async-done(((bf16[2,24,1536]{2,1,0:T(8,128)(2,1)}), bf16[2,384,1536]{2,1,0:T(8,128)(2,1)}) %all-gather.4.cloned.1.call-update) | async-done | bytes 2359312 | tf_op jit(solution)/shard_map/all_gather | solution.py:67
  55.3 2.8 %fusion.23 = (bf16[1,384,1536]{2,1,0:T(8,128)(2,1)}, bf16[1,384,1536]{2,1,0:T(8,128)(2,1)S(1)}) fusion(bf16[2,384,1536]{2,1,0:T(8,128)(2,1)} %all-gather.4.cloned.1.call-done), kind=kLoop, calls=%fused_computation.43 | loop fusion | bytes 4718592 | tf_op jit(solution)/shard_map/slice | solution.py:31
  58.1 1.7 copy.25
  59.8 1.4 copy.27
  61.2 0.0 copy-start.3
  61.2 1.4 fusion.26
  62.6 0.3 fusion.8
  63.0 0.0 copy-done.3
  63.0 0.6 fusion.6
  63.6 0.8 reshape.71
  64.4 34.8 %all-gather.6.cloned.1.call-done = bf16[2,384,1536]{2,1,0:T(8,128)(2,1)} async-done(((bf16[2,24,1536]{2,1,0:T(8,128)(2,1)}), bf16[2,384,1536]{2,1,0:T(8,128)(2,1)}) %all-gather.6.cloned.1.call-update) | async-done | bytes 2359312 | tf_op jit(solution)/shard_map/all_gather | solution.py:70
  99.2 2.8 %fusion.24 = (bf16[1,384,1536]{2,1,0:T(8,128)(2,1)}, bf16[1,384,1536]{2,1,0:T(8,128)(2,1)S(1)}) fusion(bf16[2,384,1536]{2,1,0:T(8,128)(2,1)} %all-gather.6.cloned.1.call-done), kind=kLoop, calls=%fused_computation.44 | loop fusion | bytes 4718592 | tf_op jit(solution)/shard_map/slice | solution.py:31
  102.0 1.7 copy.29
  103.7 1.3 fusion.25
  105.0 0.0 copy-start.1
  105.0 0.9 copy-done.1
  106.0 0.3 fusion.10
  106.3 0.0 copy-start.2
  106.3 1.4 copy.31
  107.7 0.0 copy-done.2
  107.7 0.0 copy-start.5
  107.7 1.9 %fusion.7 = bf16[24,24,64]{2,0,1:T(8,128)(2,1)S(1)} fusion(bf16[384,24,64]{0,2,1:T(8,128)(2,1)} %bitcast.42, f32[24,24,384]{2,0,1:T(8,128)S(1)} %copy-done.2, f32[24,24]{0,1:T(8,128)S(1)} %get-tuple-element.15, f32[24,24]{0,1:T(8,128)S(1)} %get-tuple-element.14, f32[24,24]{0,1:T(8,128)S(1)} %get-tuple-element.13), kind=kOutput, calls=%fused_computation.11 | convolution fusion | flops 28864512 | bytes 2145024 | tf_op jit(solution)/shard_map/qhk,khd->qhd/dot_general | solution.py:40
  109.7 0.2 reshape.72
  109.8 0.0 copy-done.5
  109.8 0.7 pad_maximum_fusion
  110.5 0.0 all-gather.8.cloned.1.call-update
  111.3 40.3 %all-gather.8.cloned.1.call-done = bf16[384,3072]{1,0:T(8,128)(2,1)} async-done(((bf16[24,3072]{1,0:T(8,128)(2,1)}), bf16[384,3072]{1,0:T(8,128)(2,1)}) %all-gather.8.cloned.1.call-update) | async-done | bytes 2359312 | tf_op jit(solution)/shard_map/all_gather | solution.py:74
  151.7 0.0 copy-done
  151.7 2.6 %convolution_convert_fusion = bf16[384,192]{0,1:T(8,128)(2,1)S(1)} fusion(bf16[384,3072]{1,0:T(8,128)(2,1)} %all-gather.8.cloned.1.call-done, bf16[3072,192]{0,1:T(8,128)(2,1)S(1)} %copy-done), kind=kOutput, calls=%fused_computation.12 | convolution fusion | flops 453058560 | bytes 3686400 | tf_op jit(solution)/shard_map/dot_general | solution.py:73
  154.3 0.8 copy.33
  155.1 3.5 %all-to-all-start = ((bf16[16,24,192]{2,1,0:T(8,128)(2,1)}), bf16[16,24,192]{2,1,0:T(8,128)(2,1)S(1)}, u32[]{:S(2)}, u32[]{:S(2)}) async-start(bf16[16,24,192]{2,1,0:T(8,128)(2,1)} %bitcast.8), calls=%async_computation | async-start | bytes 393216 | tf_op jit(solution)/shard_map/all_to_all | solution.py:78
  158.6 3.7 %fusion.27 = f32[1,6144]{1,0:T(1,128)S(1)} fusion(bf16[512,1]{0,1:T(2,128)(2,1)S(1)} %reshape.77, bf16[512,6144]{1,0:T(8,128)(2,1)} %param.14), kind=kOutput, calls=%fused_computation.47 | convolution fusion | flops 6291456 | bytes 6317056 | tf_op jit(solution)/shard_map/dot_general | solution.py:84
  162.4 0.0 copy-start.4
  162.5 5.2 %all-to-all-done = bf16[16,24,192]{2,1,0:T(8,128)(2,1)S(1)} async-done(((bf16[16,24,192]{2,1,0:T(8,128)(2,1)}), bf16[16,24,192]{2,1,0:T(8,128)(2,1)S(1)}, u32[]{:S(2)}, u32[]{:S(2)}) %all-to-all-start) | async-done | bytes 147488 | tf_op jit(solution)/shard_map/all_to_all | solution.py:78
  167.6 0.0 copy-start.6
  167.7 0.0 copy-start.7
  167.7 0.1 copy.34
  167.8 0.2 reshape.73
  168.0 0.0 copy-done.4
  168.0 0.2 fusion.19
  168.1 0.8 multiply_reduce_fusion
  168.9 0.0 copy-done.6
  169.0 0.0 copy-done.7
  169.0 0.9 multiply_add_fusion
  (11 shorter events, 0.2 us)
Async XLA Ops:
  7.2 144.5 %copy-start = (bf16[3072,192]{0,1:T(8,128)(2,1)S(1)}, bf16[3072,192]{0,1:T(8,128)(2,1)}, u32[]{:S(2)}) copy-start(bf16[3072,192]{0,1:T(8,128)(2,1)} %param.13) | copy-start | bytes 3538948
  7.2 3.5 %slice-start.1 = ((bf16[3,24,1536]{2,1,0:T(8,128)(2,1)}), bf16[1,24,1536]{2,1,0:T(8,128)(2,1)S(1)}, s32[]{:S(2)}) async-start(bf16[3,24,1536]{2,1,0:T(8,128)(2,1)} %param.10), calls=%async_computation.5 | async-start | bytes 147456 | tf_op jit(solution)/shard_map/slice | solution.py:57
  7.2 4.3 %slice-start = ((bf16[3,24,1536]{2,1,0:T(8,128)(2,1)}), bf16[1,24,1536]{2,1,0:T(8,128)(2,1)S(1)}, s32[]{:S(2)}) async-start(bf16[3,24,1536]{2,1,0:T(8,128)(2,1)} %param.11), calls=%async_computation.4 | async-start | bytes 147456 | tf_op jit(solution)/shard_map/slice | solution.py:58
  7.2 48.1 %all-gather.4.cloned.1.call-start = ((), (), s32[]{:S(2)}) async-start(), calls=%async_computation.1 | async-start | bytes 2506752 | tf_op jit(solution)/shard_map/all_gather | solution.py:67
  8.9 90.3 %all-gather.6.cloned.1.call-start = ((), (), s32[]{:S(2)}) async-start(), calls=%async_computation.2 | async-start | bytes 2506752 | tf_op jit(solution)/shard_map/all_gather | solution.py:70
  10.6 141.1 %all-gather.8.cloned.1.call-start = ((), (), s32[]{:S(2)}) async-start(), calls=%async_computation.3 | async-start | bytes 2506752 | tf_op jit(solution)/shard_map/all_gather | solution.py:74
  61.2 1.8 copy-start.3
  105.0 0.9 copy-start.1
  106.3 1.4 copy-start.2
  107.7 2.1 %copy-start.5 = (bf16[24,1536]{1,0:T(8,128)(2,1)S(1)}, bf16[24,1536]{1,0:T(8,128)(2,1)}, u32[]{:S(2)}) copy-start(bf16[24,1536]{1,0:T(8,128)(2,1)} %reshape.71) | copy-start | bytes 221188
  155.1 12.5 %all-to-all-start = ((bf16[16,24,192]{2,1,0:T(8,128)(2,1)}), bf16[16,24,192]{2,1,0:T(8,128)(2,1)S(1)}, u32[]{:S(2)}, u32[]{:S(2)}) async-start(bf16[16,24,192]{2,1,0:T(8,128)(2,1)} %bitcast.8), calls=%async_computation | async-start | bytes 393216 | tf_op jit(solution)/shard_map/all_to_all | solution.py:78
  162.4 5.6 %copy-start.4 = (bf16[24,3072]{1,0:T(8,128)(2,1)S(1)}, bf16[24,3072]{1,0:T(8,128)(2,1)}, u32[]{:S(2)}) copy-start(bf16[24,3072]{1,0:T(8,128)(2,1)} %param.8) | copy-start | bytes 442372
  167.6 1.3 copy-start.6
  167.7 1.3 copy-start.7
Sparse Core Ops, SparseCore 0:
  10.3 44.9 all-gather.3
  58.2 41.0 all-gather.5
  110.6 40.9 all-gather.7
where the time goes:
time: 177 us; the launch traced here: 176 us
  waiting for transfers between devices  123 us (69%)
  local copies, waits for them, and re-layouts  19.7 us (11%)
  between operations  14.8 us (8%)
  matrix products  12.4 us (7%)
  starting transfers between devices  3.64 us (2%)
  other arithmetic  2.4 us (1%)
    all_gather x1, waiting for transfers between devices, local(): lax.all_gather(base_pairs, 'seq', axis=1, tiled=True)  43 us
    all_gather x1, waiting for transfers between devices, local(): lax.all_gather(joined, 'seq', axis=0, tiled=True)  40.3 us
    all_gather x1, waiting for transfers between devices, local(): lax.all_gather(control_pairs, 'seq', axis=1, tiled=True)  34.8 us
    slice x4, local copies, waits for them, and re-layouts, attend(): keys_block = shard_rows[0].reshape(count, HEADS, HD)  9.01 us
    all_to_all x1, waiting for transfers between devices, local(): lax.all_to_all(column_part.astype(jnp.bfloat16), 'seq', split_axis=0, con...  5.15 us
    dot_general x1, matrix products, local(): jnp.dot(embedding[None, :], w_mod, preferred_element_type=jnp.float32)[0]  3.71 us
  transfers between devices with their start and end apart: 4, of which 4 were waited for; matrix products, arithmetic and copies ran while one was open for 9% of the time, Pallas kernels for 0%

commit v1 on v0

--- a/solution.py
+++ b/solution.py
@@ -1,8 +1,11 @@
+import functools
 import math
 
 import jax
 import jax.numpy as jnp
 from jax import lax
+from jax.experimental import pallas as pl
+from jax.experimental.pallas import tpu as pltpu
 from jax.sharding import PartitionSpec as P
 
 D = 3072
@@ -52,7 +55,7 @@
     return outputs.reshape(outputs.shape[0], HEADS * HD)
 
 
-def local(hidden, latents, base_qkv, control_qkv, step_index, w_join, w_mod, w_out):
+def gathered(hidden, latents, base_qkv, control_qkv, step_index, w_join, w_mod, w_out):
     tokens_here = hidden.shape[0]
     base_queries = base_qkv[0].reshape(tokens_here, HEADS, HD)
     control_queries = control_qkv[0].reshape(tokens_here, HEADS, HD)
@@ -95,6 +98,444 @@
     return (hidden_next, velocity, latents_next)
 
 
+LANES = 128
+MESH = pl.DeviceIdType.MESH
+
+
+def fused_kernel(
+    plan,
+    hidden_in,
+    latents_in,
+    base_in,
+    control_in,
+    step_in,
+    join_in,
+    mod_in,
+    out_in,
+    next_ref,
+    velocity_ref,
+    latents_ref,
+    hidden,
+    latents,
+    w_out,
+    w_mod,
+    w_join,
+    modulation,
+    heads_own,
+    heads_other,
+    joined,
+    total,
+    update_out,
+    update_in,
+    summed,
+    load_sem,
+    own_sem,
+    swap_send,
+    swap_recv,
+    pass_send,
+    pass_recv,
+    side_send,
+    side_recv,
+    right_send,
+    left_send,
+    cross_send,
+    join_recv,
+    back_send,
+    back_recv,
+):
+    chips, rows, lines, width, pieces = plan
+    tokens = hidden.shape[0]
+    section = base_in.shape[2]
+    per_section = section // width
+    me = lax.axis_index("seq")
+    core = lax.rem(me, 2)
+    chip = me // 2
+    row = lax.rem(chip, rows)
+    place = chip // rows
+
+    def device(other, other_core):
+        return {"seq": other * 2 + other_core}
+
+    def remote(src, dst, send, recv, target):
+        return pltpu.make_async_remote_copy(
+            src_ref=src,
+            dst_ref=dst,
+            send_sem=send,
+            recv_sem=recv,
+            device_id=target,
+            device_id_type=MESH,
+        )
+
+    mod_load = pltpu.make_async_copy(mod_in, w_mod, load_sem.at[0])
+    small_loads = [
+        pltpu.make_async_copy(hidden_in, hidden, load_sem.at[1]),
+        pltpu.make_async_copy(latents_in, latents, load_sem.at[2]),
+        pltpu.make_async_copy(out_in, w_out, load_sem.at[3]),
+        pltpu.make_async_copy(join_in, w_join.at[core], load_sem.at[4]),
+    ]
+    barrier = pltpu.get_barrier_semaphore()
+    for step in range(1, chips):
+        pl.semaphore_signal(
+            barrier,
+            inc=1,
+            device_id=device(lax.rem(chip + step, chips), core),
+            device_id_type=MESH,
+        )
+    pl.semaphore_signal(barrier, inc=1, device_id=device(chip, 1 - core), device_id_type=MESH)
+    mod_load.start()
+    for load in small_loads:
+        load.start()
+    pl.semaphore_wait(barrier, chips)
+
+    def piece_of(ref, target, piece):
+        start = lax.rem(target, per_section) * width + piece * LANES
+        return ref.at[:, :, pl.ds(pl.multiple_of(start, LANES), LANES)]
+
+    def from_section(target, act):
+        @pl.when(target < per_section)
+        def _():
+            act(base_in)
+
+        @pl.when(target >= per_section)
+        def _():
+            act(control_in)
+
+    def columns(piece):
+        return pl.ds(piece * LANES, LANES)
+
+    def swap(ref, target, step, piece):
+        return remote(
+            piece_of(ref, target, piece),
+            heads_own.at[chip, :, :, columns(piece)],
+            swap_send.at[step, piece],
+            swap_recv.at[chip, piece],
+            device(target, core),
+        )
+
+    def own_copy(ref, piece):
+        return pltpu.make_async_copy(
+            piece_of(ref, chip, piece), heads_own.at[chip, :, :, columns(piece)], own_sem.at[piece]
+        )
+
+    def pass_on(source, piece):
+        return remote(
+            heads_own.at[source, 1:3, :, columns(piece)],
+            heads_other.at[source, :, :, columns(piece)],
+            pass_send.at[source, piece],
+            pass_recv.at[source, piece],
+            device(chip, 1 - core),
+        )
+
+    side = remote(join_in, w_join.at[core], side_send, side_recv, device(chip, 1 - core))
+    for piece in range(pieces):
+        for step in range(1, chips):
+            target = lax.rem(chip + step, chips)
+            from_section(
+                target, lambda ref, t=target, s=step, p=piece: swap(ref, t, s, p).start()
+            )
+        from_section(chip, lambda ref, p=piece: own_copy(ref, p).start())
+    side.start()
+
+    step_value = jnp.full((1, TEMB), step_in[0].astype(jnp.float32))
+    level_now = jnp.cos(0.5 * math.pi * step_value / STEPS)
+    level_next = jnp.cos(0.5 * math.pi * (step_value + 1.0) / STEPS)
+    half_width = TEMB // 2
+    index = lax.broadcasted_iota(jnp.int32, (1, TEMB), 1)
+    place_in_half = jnp.where(index < half_width, index, index - half_width).astype(jnp.float32)
+    frequency = jnp.exp(-math.log(10000.0) * place_in_half / half_width)
+    angles = 1000.0 * level_now * frequency
+    embedding = jnp.where(index < half_width, jnp.cos(angles), jnp.sin(angles))
+    embedding = jnp.broadcast_to(embedding, (16, TEMB)).astype(jnp.bfloat16)
+    step_size = (level_next - level_now)[:, : latents.shape[1]]
+    mod_load.wait()
+    block = 512
+    for start in range(0, w_mod.shape[1], block):
+        modulation[:, start : start + block] = jnp.dot(
+            embedding, w_mod[:, start : start + block], preferred_element_type=jnp.float32
+        )[0:1]
+
+    lane = lax.broadcasted_iota(jnp.int32, (chips * tokens, LANES), 1)
+
+    def attention(piece):
+        def rows_of(ref, kind):
+            part = ref[:, kind, :, piece * LANES : (piece + 1) * LANES].astype(jnp.float32)
+            return part.reshape(chips * tokens, LANES)
+
+        queries = rows_of(heads_own, 0) * HD ** (-0.5)
+        keys = jnp.concatenate([rows_of(heads_own, 1), rows_of(heads_other, 0)], axis=0)
+        values = jnp.concatenate([rows_of(heads_own, 2), rows_of(heads_other, 1)], axis=0)
+        keys = keys.astype(jnp.bfloat16)
+        values = values.astype(jnp.bfloat16)
+        result = None
+        for head in range(LANES // HD):
+            mine = (lane >= head * HD) & (lane < (head + 1) * HD)
+            query = jnp.where(mine, queries, 0.0).astype(jnp.bfloat16)
+            scores = lax.dot_general(
+                query, keys, (((1,), (1,)), ((), ())), preferred_element_type=jnp.float32
+            )
+            exponent = jnp.exp(scores - jnp.max(scores, axis=1, keepdims=True))
+            row_sum = jnp.sum(exponent, axis=1, keepdims=True)
+            mixed = jnp.dot(
+                exponent.astype(jnp.bfloat16), values, preferred_element_type=jnp.float32
+            )
+            mixed = mixed / row_sum
+            result = mixed if result is None else jnp.where(mine, mixed, result)
+        joined[chip, :, piece * LANES : (piece + 1) * LANES] = result.astype(jnp.bfloat16)
+
+    def hop(block_chip, piece, send, target):
+        view = joined.at[block_chip, :, columns(piece)]
+        return remote(
+            view,
+            view,
+            send.at[block_chip, piece],
+            join_recv.at[block_chip, piece],
+            device(target, core),
+        )
+
+    def other_row_step(step):
+        return lax.rem(row + step, rows)
+
+    def hand_on(origin, piece, act):
+        block_chip = origin * rows + row
+
+        @pl.when((origin <= place) & (place < lines - 1))
+        def _():
+            act(hop(block_chip, piece, right_send, chip + rows))
+
+        @pl.when((origin >= place) & (place > 0))
+        def _():
+            act(hop(block_chip, piece, left_send, chip - rows))
+
+        for step in range(1, rows):
+            act(hop(block_chip, piece, cross_send, place * rows + other_row_step(step)))
+
+    def at_distance(distance, act):
+        @pl.when(place >= distance)
+        def _():
+            act(place - distance)
+
+        @pl.when(place + distance < lines)
+        def _():
+            act(place + distance)
+
+    def arrive(block_chip, piece):
+        view = joined.at[block_chip, :, columns(piece)]
+        remote(
+            view,
+            view,
+            cross_send.at[block_chip, piece],
+            join_recv.at[block_chip, piece],
+            device(chip, 1 - core),
+        ).wait_recv()
+
+    def relay(distance, piece):
+        def act(origin):
+            arrive(origin * rows + row, piece)
+            hand_on(origin, piece, lambda copy: copy.start())
+
+        at_distance(distance, act)
+
+    for piece in range(pieces):
+        from_section(chip, lambda ref, p=piece: own_copy(ref, p).wait())
+        pass_on(chip, piece).start()
+        for step in range(1, chips):
+            source = lax.rem(chip - step + chips, chips)
+            remote(
+                heads_own.at[source, :, :, columns(piece)],
+                heads_own.at[source, :, :, columns(piece)],
+                swap_send.at[step, piece],
+                swap_recv.at[source, piece],
+                device(source, core),
+            ).wait_recv()
+            pass_on(source, piece).start()
+        for step in range(chips):
+            pass_on(lax.rem(chip - step + chips, chips), piece).wait_recv()
+        attention(piece)
+        hand_on(place, piece, lambda copy: copy.start())
+        for earlier in range(piece):
+            distance = piece - earlier
+            if distance < lines:
+                relay(distance, earlier)
+
+    small_loads[3].wait()
+    side.wait_recv()
+
+    def project(block_chip):
+        block_rows = pl.ds(pl.multiple_of(block_chip * width, width), width)
+        for half in range(2):
+            total[half] += jnp.dot(
+                joined[block_chip], w_join[half, block_rows, :], preferred_element_type=jnp.float32
+            )
+
+    total[...] = jnp.zeros_like(total)
+    project(chip)
+    done = {p: pieces - 1 - p for p in range(pieces)}
+    for distance in range(1, lines):
+        for piece in range(pieces):
+            if done[piece] < distance:
+                relay(distance, piece)
+                done[piece] = distance
+        at_distance(distance, lambda origin: project(origin * rows + row))
+        for step in range(1, rows):
+
+            def cross(origin, s=step):
+                block_chip = origin * rows + other_row_step(s)
+                for piece in range(pieces):
+                    arrive(block_chip, piece)
+                project(block_chip)
+
+            if distance == 1:
+                cross(place)
+            if distance > 1:
+                at_distance(distance - 1, cross)
+    for step in range(1, rows):
+
+        def last_cross(origin, s=step):
+            block_chip = origin * rows + other_row_step(s)
+            for piece in range(pieces):
+                arrive(block_chip, piece)
+            project(block_chip)
+
+        if lines == 1:
+            last_cross(place)
+        else:
+            at_distance(lines - 1, last_cross)
+
+    update = jnp.concatenate([total[0], total[1]], axis=1)
+    update_out[...] = update.reshape(chips, tokens, width).astype(jnp.bfloat16)
+
+    def back(target, step):
+        return remote(
+            update_out.at[target],
+            update_in.at[chip],
+            back_send.at[step],
+            back_recv.at[chip],
+            device(target, core),
+        )
+
+    for step in range(1, chips):
+        back(lax.rem(chip + step, chips), step).start()
+    update_in[chip] = update_out[chip]
+    for load in small_loads[:3]:
+        load.wait()
+    for step in range(1, chips):
+        source = lax.rem(chip - step + chips, chips)
+        remote(
+            update_out.at[source],
+            update_in.at[source],
+            back_send.at[step],
+            back_recv.at[source],
+            device(source, core),
+        ).wait_recv()
+    for source in range(chips):
+        cut = slice(source * width, (source + 1) * width)
+        summed[:, cut] = hidden[:, cut].astype(jnp.float32) + update_in[source].astype(jnp.float32)
+    whole = summed[...]
+    next_ref[...] = whole.astype(jnp.bfloat16)
+    average = jnp.mean(whole, axis=1, keepdims=True)
+    centered = whole - average
+    variance = jnp.mean(centered * centered, axis=1, keepdims=True)
+    shift_term = modulation[:, :D]
+    gain_term = modulation[:, D:]
+    normed = centered / jnp.sqrt(variance + 1e-05) * (1.0 + gain_term) + shift_term
+    velocity = jnp.dot(
+        normed.astype(jnp.bfloat16), w_out[...], preferred_element_type=jnp.float32
+    )
+    velocity_ref[...] = velocity
+    latents_ref[...] = latents[...] + step_size * velocity
+
+    for piece in range(pieces):
+        for step in range(1, chips):
+            swap(base_in, lax.rem(chip + step, chips), step, piece).wait_send()
+        for source in range(chips):
+            pass_on(source, piece).wait_send()
+        for distance in range(lines):
+            if distance == 0:
+                hand_on(place, piece, lambda copy: copy.wait_send())
+            else:
+                at_distance(
+                    distance, lambda o, p=piece: hand_on(o, p, lambda copy: copy.wait_send())
+                )
+    side.wait_send()
+    for step in range(1, chips):
+        back(lax.rem(chip + step, chips), step).wait_send()
+
+
+def fused(plan, hidden, latents, base_qkv, control_qkv, step_index, w_join, w_mod, w_out):
+    chips, rows, lines, width, pieces = plan
+    tokens = hidden.shape[0]
+    any_spec = pl.BlockSpec(memory_space=pl.ANY)
+    vmem_spec = pl.BlockSpec(memory_space=pltpu.VMEM)
+    half_columns = w_join.shape[1]
+    dma = pltpu.SemaphoreType.DMA
+    return pl.pallas_call(
+        functools.partial(fused_kernel, plan),
+        out_shape=(
+            jax.ShapeDtypeStruct(hidden.shape, jnp.bfloat16),
+            jax.ShapeDtypeStruct(latents.shape, jnp.float32),
+            jax.ShapeDtypeStruct(latents.shape, jnp.float32),
+        ),
+        in_specs=[any_spec] * 4
+        + [pl.BlockSpec(memory_space=pltpu.SMEM)]
+        + [any_spec] * 3,
+        out_specs=(vmem_spec,) * 3,
+        scratch_shapes=[
+            pltpu.VMEM(hidden.shape, jnp.bfloat16),
+            pltpu.VMEM(latents.shape, jnp.float32),
+            pltpu.VMEM(w_out.shape, jnp.bfloat16),
+            pltpu.VMEM(w_mod.shape, jnp.bfloat16),
+            pltpu.VMEM((2,) + w_join.shape, jnp.bfloat16),
+            pltpu.VMEM((1, w_mod.shape[1]), jnp.float32),
+            pltpu.VMEM((chips, 3, tokens, width), jnp.bfloat16),
+            pltpu.VMEM((chips, 2, tokens, width), jnp.bfloat16),
+            pltpu.VMEM((chips, chips * tokens, width), jnp.bfloat16),
+            pltpu.VMEM((2, chips * tokens, half_columns), jnp.float32),
+            pltpu.VMEM((chips, tokens, width), jnp.bfloat16),
+            pltpu.VMEM((chips, tokens, width), jnp.bfloat16),
+            pltpu.VMEM(hidden.shape, jnp.float32),
+            dma((5,)),
+            dma((pieces,)),
+            dma((chips, pieces)),
+            dma((chips, pieces)),
+            dma((chips, pieces)),
+            dma((chips, pieces)),
+            dma,
+            dma,
+            dma((chips, pieces)),
+            dma((chips, pieces)),
+            dma((chips, pieces)),
+            dma((chips, pieces)),
+            dma((chips,)),
+            dma((chips,)),
+        ],
+        compiler_params=pltpu.CompilerParams(
+            collective_id=0, has_side_effects=True, vmem_limit_bytes=48 * 1024 * 1024
+        ),
+        name="fused",
+    )(hidden, latents, base_qkv, control_qkv, step_index, w_join, w_mod, w_out)
+
+
+def plan_for(count, sections_width, section_width):
+    if count % 4 != 0:
+        return None
+    chips = count // 2
+    width = sections_width // chips
+    if sections_width % chips or width % LANES or section_width % width:
+        return None
+    return (chips, 2, chips // 2, width, width // LANES)
+
+
+def local(hidden, latents, base_qkv, control_qkv, step_index, w_join, w_mod, w_out, count):
+    plan = plan_for(count, w_join.shape[0], base_qkv.shape[2])
+    if plan is None or hidden.shape[0] % 8 or (plan[0] * hidden.shape[0]) % 16:
+        return gathered(
+            hidden, latents, base_qkv, control_qkv, step_index, w_join, w_mod, w_out
+        )
+    return fused(
+        plan, hidden, latents, base_qkv, control_qkv, step_index, w_join, w_mod, w_out
+    )
+
+
 def solution(mesh):
     in_specs = (
         P(("groups", "seq"), None),
@@ -107,4 +548,10 @@
         P(),
     )
     out_specs = (P(("groups", "seq"), None), P(("groups", "seq"), None), P(("groups", "seq"), None))
-    return jax.shard_map(local, mesh=mesh, in_specs=in_specs, out_specs=out_specs, check_vma=False)
+    return jax.shard_map(
+        functools.partial(local, count=mesh.shape["seq"]),
+        mesh=mesh,
+        in_specs=in_specs,
+        out_specs=out_specs,
+        check_vma=False,
+    )

time: 177 us -> 46.1 us (0.26)
  waiting for transfers between devices: 123 us -> 0 us
  Pallas kernels: 0 us -> 39.6 us
  local copies, waits for them, and re-layouts: 19.7 us -> 4.96 us
  between operations: 14.8 us -> 1.36 us
  matrix products: 12.4 us -> 0 us
  starting transfers between devices: 3.64 us -> 0 us
  other arithmetic: 2.4 us -> 0 us
    all_gather x3 -> x0, waiting for transfers between devices: 118 us -> none  [the longest x1 43 us: local(): lax.all_gather(base_pairs, 'seq', axis=1, tiled=True)]
    pallas_call x0 -> x1, Pallas kernels: none -> 39.6 us  [fused(): pl.pallas_call(functools.partial(fused_kernel, plan), out_shape=(jax.Shap...]
    slice x12 -> x0, local copies, waits for them, and re-layouts: 15.1 us -> none  [the longest x4 9.01 us: attend(): keys_block = shard_rows[0].reshape(count, HEADS, HD)]
    dot_general x7 -> x0, matrix products: 12.4 us -> none  [the longest x1 3.71 us: local(): jnp.dot(embedding[None, :], w_mod, preferred_element_type=jnp.float32)[0]]
    all_to_all x1 -> x0, waiting for transfers between devices: 5.15 us -> none  [local(): lax.all_to_all(column_part.astype(jnp.bfloat16), 'seq', split_axis=0, con...]
    unnamed x16 -> x13, local copies, waits for them, and re-layouts: 0.95 us -> 4.96 us
    all_to_all x1 -> x0, starting transfers between devices: 3.52 us -> none  [local(): lax.all_to_all(column_part.astype(jnp.bfloat16), 'seq', split_axis=0, con...]
  transfers between devices with their start and end apart: 4 -> 0, of which waited for: 4 -> 0; matrix products, arithmetic and copies ran while one was open for 9% -> 0% of each run, Pallas kernels for 0% -> 0%
where the time goes in v1:
time: 46.1 us; the launch traced here: 45.9 us
  Pallas kernels  39.6 us (86%)
  local copies, waits for them, and re-layouts  4.96 us (11%)
  between operations  1.36 us (3%)
    pallas_call x1, Pallas kernels, fused(): pl.pallas_call(functools.partial(fused_kernel, plan), out_shape=(jax.Shap...  39.6 us
    unnamed x13, local copies, waits for them, and re-layouts  4.96 us

profile of v1, /device:TPU:0, one launch (start us, length us, event | category | flops | bytes accessed | tf_op | source)
XLA Modules:
  0.0 45.9 jit_solution(2629369143018631915)
XLA Ops:
  1.3 1.4 %copy.12.out_in = bf16[3072,64]{1,0:T(8,128)(2,1)S(1)} copy(bf16[3072,64]{0,1:T(8,128)(2,1)} %param.15) | data formatting | bytes 786432 | tf_op args[7]
  2.7 0.0 copy-start
  2.7 0.0 copy-start.1
  2.7 0.0 copy-start.2
  2.7 0.0 copy-start.3
  2.7 1.7 %copy.11.join_in = bf16[3072,192]{1,0:T(8,128)(2,1)S(1)} copy(bf16[3072,192]{0,1:T(8,128)(2,1)} %param.13) | data formatting | bytes 2359296 | tf_op args[5]
  4.4 0.0 copy-done
  4.4 0.0 copy-done.1
  4.4 0.0 copy-done.2
  4.4 0.0 copy-done.3
  4.5 39.6 %fused.1 = (bf16[24,3072]{1,0:T(8,128)(2,1)S(1)}, f32[24,64]{1,0:T(8,128)S(1)}, f32[24,64]{1,0:T(8,128)S(1)}) custom-call(bf16[24,3072]{1,0:T(8,128)(2,1)S(1)} %copy-done.2, f32[24,64]{1,0:T(8,128)S(1)} %copy-done.3, bf16[3,24,1536]{2,1,0:T(8,128)(2,1)S(1)} %copy-done, bf16[3,24,1536]{2,1,0:T(8,128)(2,1)S(1)} %copy-done.1, s32[1]{0:T(128)S(6)} %copy.16.step_in, ...), custom_call_target="tpu_custom_call" | custom-call | tf_op jit(solution)/shard_map/fused/pallas_call | solution.py:471
  44.0 0.7 %copy.17 = bf16[24,3072]{1,0:T(8,128)(2,1)} copy(bf16[24,3072]{1,0:T(8,128)(2,1)S(1)} %get-tuple-element.6) | data formatting | bytes 294912
  44.7 0.6 %copy.18 = f32[24,64]{1,0:T(8,128)} copy(f32[24,64]{1,0:T(8,128)S(1)} %get-tuple-element.7) | data formatting | bytes 12288
  45.3 0.6 %copy.19 = f32[24,64]{1,0:T(8,128)} copy(f32[24,64]{1,0:T(8,128)S(1)} %get-tuple-element.8) | data formatting | bytes 12288
Async XLA Ops:
  2.7 1.8 %copy-start = (bf16[3,24,1536]{2,1,0:T(8,128)(2,1)S(1)}, bf16[3,24,1536]{2,1,0:T(8,128)(2,1)}, u32[]{:S(2)}) copy-start(bf16[3,24,1536]{2,1,0:T(8,128)(2,1)} %base_in.1) | copy-start | bytes 663556
  2.7 1.8 %copy-start.1 = (bf16[3,24,1536]{2,1,0:T(8,128)(2,1)S(1)}, bf16[3,24,1536]{2,1,0:T(8,128)(2,1)}, u32[]{:S(2)}) copy-start(bf16[3,24,1536]{2,1,0:T(8,128)(2,1)} %control_in.1) | copy-start | bytes 663556
  2.7 1.8 %copy-start.2 = (bf16[24,3072]{1,0:T(8,128)(2,1)S(1)}, bf16[24,3072]{1,0:T(8,128)(2,1)}, u32[]{:S(2)}) copy-start(bf16[24,3072]{1,0:T(8,128)(2,1)} %hidden_in.1) | copy-start | bytes 442372
  2.7 1.8 %copy-start.3 = (f32[24,64]{1,0:T(8,128)S(1)}, f32[24,64]{1,0:T(8,128)}, u32[]{:S(2)}) copy-start(f32[24,64]{1,0:T(8,128)} %latents_in.1) | copy-start | bytes 18436

commit v2 on v1

--- a/solution.py
+++ b/solution.py
@@ -166,12 +166,17 @@
             device_id_type=MESH,
         )
 
+    half_rows = join_in.shape[0]
+
+    def join_half(which):
+        return w_join.at[pl.ds(pl.multiple_of(which * half_rows, half_rows), half_rows), :]
+
     mod_load = pltpu.make_async_copy(mod_in, w_mod, load_sem.at[0])
     small_loads = [
         pltpu.make_async_copy(hidden_in, hidden, load_sem.at[1]),
         pltpu.make_async_copy(latents_in, latents, load_sem.at[2]),
         pltpu.make_async_copy(out_in, w_out, load_sem.at[3]),
-        pltpu.make_async_copy(join_in, w_join.at[core], load_sem.at[4]),
+        pltpu.make_async_copy(join_in, join_half(core), load_sem.at[4]),
     ]
     barrier = pltpu.get_barrier_semaphore()
     for step in range(1, chips):
@@ -185,57 +190,6 @@
     mod_load.start()
     for load in small_loads:
         load.start()
-    pl.semaphore_wait(barrier, chips)
-
-    def piece_of(ref, target, piece):
-        start = lax.rem(target, per_section) * width + piece * LANES
-        return ref.at[:, :, pl.ds(pl.multiple_of(start, LANES), LANES)]
-
-    def from_section(target, act):
-        @pl.when(target < per_section)
-        def _():
-            act(base_in)
-
-        @pl.when(target >= per_section)
-        def _():
-            act(control_in)
-
-    def columns(piece):
-        return pl.ds(piece * LANES, LANES)
-
-    def swap(ref, target, step, piece):
-        return remote(
-            piece_of(ref, target, piece),
-            heads_own.at[chip, :, :, columns(piece)],
-            swap_send.at[step, piece],
-            swap_recv.at[chip, piece],
-            device(target, core),
-        )
-
-    def own_copy(ref, piece):
-        return pltpu.make_async_copy(
-            piece_of(ref, chip, piece), heads_own.at[chip, :, :, columns(piece)], own_sem.at[piece]
-        )
-
-    def pass_on(source, piece):
-        return remote(
-            heads_own.at[source, 1:3, :, columns(piece)],
-            heads_other.at[source, :, :, columns(piece)],
-            pass_send.at[source, piece],
-            pass_recv.at[source, piece],
-            device(chip, 1 - core),
-        )
-
-    side = remote(join_in, w_join.at[core], side_send, side_recv, device(chip, 1 - core))
-    for piece in range(pieces):
-        for step in range(1, chips):
-            target = lax.rem(chip + step, chips)
-            from_section(
-                target, lambda ref, t=target, s=step, p=piece: swap(ref, t, s, p).start()
-            )
-        from_section(chip, lambda ref, p=piece: own_copy(ref, p).start())
-    side.start()
-
     step_value = jnp.full((1, TEMB), step_in[0].astype(jnp.float32))
     level_now = jnp.cos(0.5 * math.pi * step_value / STEPS)
     level_next = jnp.cos(0.5 * math.pi * (step_value + 1.0) / STEPS)
@@ -247,6 +201,59 @@
     embedding = jnp.where(index < half_width, jnp.cos(angles), jnp.sin(angles))
     embedding = jnp.broadcast_to(embedding, (16, TEMB)).astype(jnp.bfloat16)
     step_size = (level_next - level_now)[:, : latents.shape[1]]
+    pl.semaphore_wait(barrier, chips)
+
+    def piece_of(ref, target, piece):
+        start = lax.rem(target, per_section) * width + piece * LANES
+        return ref.at[:, :, pl.ds(pl.multiple_of(start, LANES), LANES)]
+
+    def from_section(target, act):
+        @pl.when(target < per_section)
+        def _():
+            act(base_in)
+
+        @pl.when(target >= per_section)
+        def _():
+            act(control_in)
+
+    def columns(piece):
+        return pl.ds(piece * LANES, LANES)
+
+    far_first = sorted(range(1, chips), key=lambda step: abs(2 * step - chips))
+
+    def swap(ref, target, step, piece):
+        return remote(
+            piece_of(ref, target, piece),
+            heads_own.at[chip, :, :, columns(piece)],
+            swap_send.at[step, piece],
+            swap_recv.at[chip, piece],
+            device(target, core),
+        )
+
+    def own_copy(ref, piece):
+        return pltpu.make_async_copy(
+            piece_of(ref, chip, piece), heads_own.at[chip, :, :, columns(piece)], own_sem.at[piece]
+        )
+
+    def pass_on(source, piece):
+        return remote(
+            heads_own.at[source, 1:3, :, columns(piece)],
+            heads_other.at[source, :, :, columns(piece)],
+            pass_send.at[source, piece],
+            pass_recv.at[source, piece],
+            device(chip, 1 - core),
+        )
+
+    side = remote(join_in, join_half(core), side_send, side_recv, device(chip, 1 - core))
+    for piece in range(pieces):
+        for step in far_first:
+            target = lax.rem(chip + step, chips)
+            from_section(
+                target, lambda ref, t=target, s=step, p=piece: swap(ref, t, s, p).start()
+            )
+        from_section(chip, lambda ref, p=piece: own_copy(ref, p).start())
+    side.start()
+
     mod_load.wait()
     block = 512
     for start in range(0, w_mod.shape[1], block):
@@ -338,7 +345,7 @@
     for piece in range(pieces):
         from_section(chip, lambda ref, p=piece: own_copy(ref, p).wait())
         pass_on(chip, piece).start()
-        for step in range(1, chips):
+        for step in reversed(far_first):
             source = lax.rem(chip - step + chips, chips)
             remote(
                 heads_own.at[source, :, :, columns(piece)],
@@ -361,11 +368,13 @@
     side.wait_recv()
 
     def project(block_chip):
-        block_rows = pl.ds(pl.multiple_of(block_chip * width, width), width)
-        for half in range(2):
-            total[half] += jnp.dot(
-                joined[block_chip], w_join[half, block_rows, :], preferred_element_type=jnp.float32
-            )
+        block_columns = pl.ds(pl.multiple_of(block_chip * width, LANES), width)
+        total[...] += lax.dot_general(
+            joined[block_chip],
+            w_join[:, block_columns],
+            (((1,), (1,)), ((), ())),
+            preferred_element_type=jnp.float32,
+        )
 
     total[...] = jnp.zeros_like(total)
     project(chip)
@@ -401,8 +410,7 @@
         else:
             at_distance(lines - 1, last_cross)
 
-    update = jnp.concatenate([total[0], total[1]], axis=1)
-    update_out[...] = update.reshape(chips, tokens, width).astype(jnp.bfloat16)
+    update_out[...] = total[...].reshape(chips, tokens, width).astype(jnp.bfloat16)
 
     def back(target, step):
         return remote(
@@ -413,7 +421,7 @@
             device(target, core),
         )
 
-    for step in range(1, chips):
+    for step in far_first:
         back(lax.rem(chip + step, chips), step).start()
     update_in[chip] = update_out[chip]
     for load in small_loads[:3]:
@@ -438,8 +446,11 @@
     shift_term = modulation[:, :D]
     gain_term = modulation[:, D:]
     normed = centered / jnp.sqrt(variance + 1e-05) * (1.0 + gain_term) + shift_term
-    velocity = jnp.dot(
-        normed.astype(jnp.bfloat16), w_out[...], preferred_element_type=jnp.float32
+    velocity = lax.dot_general(
+        normed.astype(jnp.bfloat16),
+        w_out[...],
+        (((1,), (1,)), ((), ())),
+        preferred_element_type=jnp.float32,
     )
     velocity_ref[...] = velocity
     latents_ref[...] = latents[...] + step_size * velocity
@@ -466,7 +477,6 @@
     tokens = hidden.shape[0]
     any_spec = pl.BlockSpec(memory_space=pl.ANY)
     vmem_spec = pl.BlockSpec(memory_space=pltpu.VMEM)
-    half_columns = w_join.shape[1]
     dma = pltpu.SemaphoreType.DMA
     return pl.pallas_call(
         functools.partial(fused_kernel, plan),
@@ -482,14 +492,14 @@
         scratch_shapes=[
             pltpu.VMEM(hidden.shape, jnp.bfloat16),
             pltpu.VMEM(latents.shape, jnp.float32),
-            pltpu.VMEM(w_out.shape, jnp.bfloat16),
+            pltpu.VMEM(w_out.shape[::-1], jnp.bfloat16),
             pltpu.VMEM(w_mod.shape, jnp.bfloat16),
-            pltpu.VMEM((2,) + w_join.shape, jnp.bfloat16),
+            pltpu.VMEM((2 * w_join.shape[1], w_join.shape[0]), jnp.bfloat16),
             pltpu.VMEM((1, w_mod.shape[1]), jnp.float32),
             pltpu.VMEM((chips, 3, tokens, width), jnp.bfloat16),
             pltpu.VMEM((chips, 2, tokens, width), jnp.bfloat16),
             pltpu.VMEM((chips, chips * tokens, width), jnp.bfloat16),
-            pltpu.VMEM((2, chips * tokens, half_columns), jnp.float32),
+            pltpu.VMEM((chips * tokens, width), jnp.float32),
             pltpu.VMEM((chips, tokens, width), jnp.bfloat16),
             pltpu.VMEM((chips, tokens, width), jnp.bfloat16),
             pltpu.VMEM(hidden.shape, jnp.float32),
@@ -512,7 +522,7 @@
             collective_id=0, has_side_effects=True, vmem_limit_bytes=48 * 1024 * 1024
         ),
         name="fused",
-    )(hidden, latents, base_qkv, control_qkv, step_index, w_join, w_mod, w_out)
+    )(hidden, latents, base_qkv, control_qkv, step_index, w_join.T, w_mod, w_out.T)
 
 
 def plan_for(count, sections_width, section_width):

time: 46.1 us -> 49.5 us (1.074)
  local copies, waits for them, and re-layouts: 4.96 us -> 7.61 us
  Pallas kernels: 39.6 us -> 40.3 us
    unnamed x13 -> x15, local copies, waits for them, and re-layouts: 4.96 us -> 7.61 us
    pallas_call x1, Pallas kernels: 39.6 us -> 40.3 us  [fused(): pl.pallas_call(functools.partial(fused_kernel, plan), out_shape=(jax.Shap...]
where the time goes in v2:
time: 49.5 us; the launch traced here: 49.2 us
  Pallas kernels  40.3 us (81%)
  local copies, waits for them, and re-layouts  7.61 us (15%)
  between operations  1.3 us (3%)
    pallas_call x1, Pallas kernels, fused(): pl.pallas_call(functools.partial(fused_kernel, plan), out_shape=(jax.Shap...  40.3 us
    unnamed x15, local copies, waits for them, and re-layouts  7.61 us

profile of v2, /device:TPU:0, one launch (start us, length us, event | category | flops | bytes accessed | tf_op | source)
XLA Modules:
  0.0 49.2 jit_solution(14832821498210000286)
XLA Ops:
  1.3 0.0 copy-start
  1.3 1.3 %copy-done = bf16[3072,192]{0,1:T(8,128)(2,1)S(1)} copy-done((bf16[3072,192]{0,1:T(8,128)(2,1)S(1)}, bf16[3072,192]{0,1:T(8,128)(2,1)}, u32[]{:S(2)}) %copy-start) | copy-done | bytes 1179672
  2.5 0.0 copy-start.1
  2.6 1.0 %copy-done.1 = bf16[3072,64]{0,1:T(8,128)(2,1)S(1)} copy-done((bf16[3072,64]{0,1:T(8,128)(2,1)S(1)}, bf16[3072,64]{0,1:T(8,128)(2,1)}, u32[]{:S(2)}) %copy-start.1) | copy-done | bytes 393240
  3.5 0.0 copy-start.2
  3.5 0.9 %copy-done.2 = bf16[3,24,1536]{2,1,0:T(8,128)(2,1)S(1)} copy-done((bf16[3,24,1536]{2,1,0:T(8,128)(2,1)S(1)}, bf16[3,24,1536]{2,1,0:T(8,128)(2,1)}, u32[]{:S(2)}) %copy-start.2) | copy-done | bytes 221208
  4.5 0.0 copy-start.3
  4.5 0.9 %copy-done.3 = bf16[3,24,1536]{2,1,0:T(8,128)(2,1)S(1)} copy-done((bf16[3,24,1536]{2,1,0:T(8,128)(2,1)S(1)}, bf16[3,24,1536]{2,1,0:T(8,128)(2,1)}, u32[]{:S(2)}) %copy-start.3) | copy-done | bytes 221208
  5.4 0.0 copy-start.4
  5.4 0.9 %copy-done.4 = bf16[24,3072]{1,0:T(8,128)(2,1)S(1)} copy-done((bf16[24,3072]{1,0:T(8,128)(2,1)S(1)}, bf16[24,3072]{1,0:T(8,128)(2,1)}, u32[]{:S(2)}) %copy-start.4) | copy-done | bytes 147480
  6.3 0.0 copy-start.5
  6.3 0.7 %copy-done.5 = f32[24,64]{1,0:T(8,128)S(1)} copy-done((f32[24,64]{1,0:T(8,128)S(1)}, f32[24,64]{1,0:T(8,128)}, u32[]{:S(2)}) %copy-start.5) | copy-done | bytes 6168
  7.0 40.3 %fused.1 = (bf16[24,3072]{1,0:T(8,128)(2,1)S(1)}, f32[24,64]{1,0:T(8,128)S(1)}, f32[24,64]{1,0:T(8,128)S(1)}) custom-call(bf16[24,3072]{1,0:T(8,128)(2,1)S(1)} %copy-done.4, f32[24,64]{1,0:T(8,128)S(1)} %copy-done.5, bf16[3,24,1536]{2,1,0:T(8,128)(2,1)S(1)} %copy-done.2, bf16[3,24,1536]{2,1,0:T(8,128)(2,1)S(1)} %copy-done.3, s32[1]{0:T(128)S(6)} %copy.14.step_in, ...), custom_call_target="tpu_custom_call" | custom-call | tf_op jit(solution)/shard_map/fused/pallas_call | solution.py:481
  47.3 0.7 %copy.15 = bf16[24,3072]{1,0:T(8,128)(2,1)} copy(bf16[24,3072]{1,0:T(8,128)(2,1)S(1)} %get-tuple-element.6) | data formatting | bytes 294912
  48.0 0.6 %copy.16 = f32[24,64]{1,0:T(8,128)} copy(f32[24,64]{1,0:T(8,128)S(1)} %get-tuple-element.7) | data formatting | bytes 12288
  48.6 0.6 %copy.17 = f32[24,64]{1,0:T(8,128)} copy(f32[24,64]{1,0:T(8,128)S(1)} %get-tuple-element.8) | data formatting | bytes 12288
Async XLA Ops:
  1.3 1.3 %copy-start = (bf16[3072,192]{0,1:T(8,128)(2,1)S(1)}, bf16[3072,192]{0,1:T(8,128)(2,1)}, u32[]{:S(2)}) copy-start(bf16[3072,192]{0,1:T(8,128)(2,1)} %param.13) | copy-start | bytes 3538948
  2.5 1.0 %copy-start.1 = (bf16[3072,64]{0,1:T(8,128)(2,1)S(1)}, bf16[3072,64]{0,1:T(8,128)(2,1)}, u32[]{:S(2)}) copy-start(bf16[3072,64]{0,1:T(8,128)(2,1)} %param.15) | copy-start | bytes 1179652
  3.5 0.9 %copy-start.2 = (bf16[3,24,1536]{2,1,0:T(8,128)(2,1)S(1)}, bf16[3,24,1536]{2,1,0:T(8,128)(2,1)}, u32[]{:S(2)}) copy-start(bf16[3,24,1536]{2,1,0:T(8,128)(2,1)} %base_in.1) | copy-start | bytes 663556
  4.5 0.9 %copy-start.3 = (bf16[3,24,1536]{2,1,0:T(8,128)(2,1)S(1)}, bf16[3,24,1536]{2,1,0:T(8,128)(2,1)}, u32[]{:S(2)}) copy-start(bf16[3,24,1536]{2,1,0:T(8,128)(2,1)} %control_in.1) | copy-start | bytes 663556
  5.4 0.9 %copy-start.4 = (bf16[24,3072]{1,0:T(8,128)(2,1)S(1)}, bf16[24,3072]{1,0:T(8,128)(2,1)}, u32[]{:S(2)}) copy-start(bf16[24,3072]{1,0:T(8,128)(2,1)} %hidden_in.1) | copy-start | bytes 442372
  6.3 0.7 %copy-start.5 = (f32[24,64]{1,0:T(8,128)S(1)}, f32[24,64]{1,0:T(8,128)}, u32[]{:S(2)}) copy-start(f32[24,64]{1,0:T(8,128)} %latents_in.1) | copy-start | bytes 18436

commit v3 on v2

--- a/solution.py
+++ b/solution.py
@@ -216,15 +216,12 @@
         def _():
             act(control_in)
 
-    def columns(piece):
-        return pl.ds(piece * LANES, LANES)
-
     far_first = sorted(range(1, chips), key=lambda step: abs(2 * step - chips))
 
     def swap(ref, target, step, piece):
         return remote(
             piece_of(ref, target, piece),
-            heads_own.at[chip, :, :, columns(piece)],
+            heads_own.at[chip, piece],
             swap_send.at[step, piece],
             swap_recv.at[chip, piece],
             device(target, core),
@@ -232,13 +229,13 @@
 
     def own_copy(ref, piece):
         return pltpu.make_async_copy(
-            piece_of(ref, chip, piece), heads_own.at[chip, :, :, columns(piece)], own_sem.at[piece]
+            piece_of(ref, chip, piece), heads_own.at[chip, piece], own_sem.at[piece]
         )
 
     def pass_on(source, piece):
         return remote(
-            heads_own.at[source, 1:3, :, columns(piece)],
-            heads_other.at[source, :, :, columns(piece)],
+            heads_own.at[source, piece, 1:3],
+            heads_other.at[source, piece],
             pass_send.at[source, piece],
             pass_recv.at[source, piece],
             device(chip, 1 - core),
@@ -265,7 +262,7 @@
 
     def attention(piece):
         def rows_of(ref, kind):
-            part = ref[:, kind, :, piece * LANES : (piece + 1) * LANES].astype(jnp.float32)
+            part = ref[:, piece, kind].astype(jnp.float32)
             return part.reshape(chips * tokens, LANES)
 
         queries = rows_of(heads_own, 0) * HD ** (-0.5)
@@ -287,10 +284,10 @@
             )
             mixed = mixed / row_sum
             result = mixed if result is None else jnp.where(mine, mixed, result)
-        joined[chip, :, piece * LANES : (piece + 1) * LANES] = result.astype(jnp.bfloat16)
+        joined[chip, piece] = result.astype(jnp.bfloat16)
 
     def hop(block_chip, piece, send, target):
-        view = joined.at[block_chip, :, columns(piece)]
+        view = joined.at[block_chip, piece]
         return remote(
             view,
             view,
@@ -326,7 +323,7 @@
             act(place + distance)
 
     def arrive(block_chip, piece):
-        view = joined.at[block_chip, :, columns(piece)]
+        view = joined.at[block_chip, piece]
         remote(
             view,
             view,
@@ -348,8 +345,8 @@
         for step in reversed(far_first):
             source = lax.rem(chip - step + chips, chips)
             remote(
-                heads_own.at[source, :, :, columns(piece)],
-                heads_own.at[source, :, :, columns(piece)],
+                heads_own.at[source, piece],
+                heads_own.at[source, piece],
                 swap_send.at[step, piece],
                 swap_recv.at[source, piece],
                 device(source, core),
@@ -370,7 +367,7 @@
     def project(block_chip):
         block_columns = pl.ds(pl.multiple_of(block_chip * width, LANES), width)
         total[...] += lax.dot_general(
-            joined[block_chip],
+            jnp.concatenate([joined[block_chip, p] for p in range(pieces)], axis=1),
             w_join[:, block_columns],
             (((1,), (1,)), ((), ())),
             preferred_element_type=jnp.float32,
@@ -475,7 +472,7 @@
 def fused(plan, hidden, latents, base_qkv, control_qkv, step_index, w_join, w_mod, w_out):
     chips, rows, lines, width, pieces = plan
     tokens = hidden.shape[0]
-    any_spec = pl.BlockSpec(memory_space=pl.ANY)
+    hbm_spec = pl.BlockSpec(memory_space=pltpu.HBM)
     vmem_spec = pl.BlockSpec(memory_space=pltpu.VMEM)
     dma = pltpu.SemaphoreType.DMA
     return pl.pallas_call(
@@ -485,9 +482,9 @@
             jax.ShapeDtypeStruct(latents.shape, jnp.float32),
             jax.ShapeDtypeStruct(latents.shape, jnp.float32),
         ),
-        in_specs=[any_spec] * 4
+        in_specs=[hbm_spec] * 4
         + [pl.BlockSpec(memory_space=pltpu.SMEM)]
-        + [any_spec] * 3,
+        + [hbm_spec] * 3,
         out_specs=(vmem_spec,) * 3,
         scratch_shapes=[
             pltpu.VMEM(hidden.shape, jnp.bfloat16),
@@ -496,9 +493,9 @@
             pltpu.VMEM(w_mod.shape, jnp.bfloat16),
             pltpu.VMEM((2 * w_join.shape[1], w_join.shape[0]), jnp.bfloat16),
             pltpu.VMEM((1, w_mod.shape[1]), jnp.float32),
-            pltpu.VMEM((chips, 3, tokens, width), jnp.bfloat16),
-            pltpu.VMEM((chips, 2, tokens, width), jnp.bfloat16),
-            pltpu.VMEM((chips, chips * tokens, width), jnp.bfloat16),
+            pltpu.VMEM((chips, pieces, 3, tokens, LANES), jnp.bfloat16),
+            pltpu.VMEM((chips, pieces, 2, tokens, LANES), jnp.bfloat16),
+            pltpu.VMEM((chips, pieces, chips * tokens, LANES), jnp.bfloat16),
             pltpu.VMEM((chips * tokens, width), jnp.float32),
             pltpu.VMEM((chips, tokens, width), jnp.bfloat16),
             pltpu.VMEM((chips, tokens, width), jnp.bfloat16),
@@ -519,7 +516,7 @@
             dma((chips,)),
         ],
         compiler_params=pltpu.CompilerParams(
-            collective_id=0, has_side_effects=True, vmem_limit_bytes=48 * 1024 * 1024
+            collective_id=0, has_side_effects=True, vmem_limit_bytes=60 * 1024 * 1024
         ),
         name="fused",
     )(hidden, latents, base_qkv, control_qkv, step_index, w_join.T, w_mod, w_out.T)

time: 49.5 us -> 47 us (0.949)
  local copies, waits for them, and re-layouts: 7.61 us -> 4.19 us
  Pallas kernels: 40.3 us -> 41.2 us
    unnamed x15 -> x3, local copies, waits for them, and re-layouts: 7.61 us -> 4.19 us
    pallas_call x1, Pallas kernels: 40.3 us -> 41.2 us  [fused(): pl.pallas_call(functools.partial(fused_kernel, plan), out_shape=(jax.Shap...]
where the time goes in v3:
time: 47 us; the launch traced here: 46.7 us
  Pallas kernels  41.2 us (88%)
  local copies, waits for them, and re-layouts  4.19 us (9%)
  between operations  1.29 us (3%)
    pallas_call x1, Pallas kernels, fused(): pl.pallas_call(functools.partial(fused_kernel, plan), out_shape=(jax.Shap...  41.2 us
    unnamed x3, local copies, waits for them, and re-layouts  4.19 us

profile of v3, /device:TPU:0, one launch (start us, length us, event | category | flops | bytes accessed | tf_op | source)
XLA Modules:
  0.0 46.7 jit_solution(4709545665730035887)
XLA Ops:
  1.3 41.2 %fused.1 = (bf16[24,3072]{1,0:T(8,128)(2,1)}, f32[24,64]{1,0:T(8,128)}, f32[24,64]{1,0:T(8,128)}) custom-call(bf16[24,3072]{1,0:T(8,128)(2,1)} %hidden_in.1, f32[24,64]{1,0:T(8,128)} %latents_in.1, bf16[3,24,1536]{2,1,0:T(8,128)(2,1)} %base_in.1, bf16[3,24,1536]{2,1,0:T(8,128)(2,1)} %control_in.1, s32[1]{0:T(128)S(6)} %copy.14.step_in, ...), custom_call_target="tpu_custom_call" | custom-call | tf_op jit(solution)/shard_map/fused/pallas_call | solution.py:478
  42.5 1.6 %copy.15 = bf16[24,3072]{1,0:T(8,128)(2,1)} copy(bf16[24,3072]{1,0:T(8,128)(2,1)} %get-tuple-element.6) | data formatting | bytes 294912
  44.1 1.3 %copy.16 = f32[24,64]{1,0:T(8,128)} copy(f32[24,64]{1,0:T(8,128)} %get-tuple-element.7) | data formatting | bytes 12288
  45.4 1.3 %copy.17 = f32[24,64]{1,0:T(8,128)} copy(f32[24,64]{1,0:T(8,128)} %get-tuple-element.8) | data formatting | bytes 12288

commit v4 on v3

--- a/solution.py
+++ b/solution.py
@@ -104,20 +104,13 @@
 
 def fused_kernel(
     plan,
-    hidden_in,
-    latents_in,
     base_in,
     control_in,
     step_in,
     join_in,
     mod_in,
-    out_in,
-    next_ref,
-    velocity_ref,
-    latents_ref,
-    hidden,
-    latents,
-    w_out,
+    update_in,
+    terms_ref,
     w_mod,
     w_join,
     modulation,
@@ -126,8 +119,6 @@
     joined,
     total,
     update_out,
-    update_in,
-    summed,
     load_sem,
     own_sem,
     swap_send,
@@ -144,7 +135,7 @@
     back_recv,
 ):
     chips, rows, lines, width, pieces = plan
-    tokens = hidden.shape[0]
+    tokens = base_in.shape[1]
     section = base_in.shape[2]
     per_section = section // width
     me = lax.axis_index("seq")
@@ -172,12 +163,7 @@
         return w_join.at[pl.ds(pl.multiple_of(which * half_rows, half_rows), half_rows), :]
 
     mod_load = pltpu.make_async_copy(mod_in, w_mod, load_sem.at[0])
-    small_loads = [
-        pltpu.make_async_copy(hidden_in, hidden, load_sem.at[1]),
-        pltpu.make_async_copy(latents_in, latents, load_sem.at[2]),
-        pltpu.make_async_copy(out_in, w_out, load_sem.at[3]),
-        pltpu.make_async_copy(join_in, join_half(core), load_sem.at[4]),
-    ]
+    join_load = pltpu.make_async_copy(join_in, join_half(core), load_sem.at[1])
     barrier = pltpu.get_barrier_semaphore()
     for step in range(1, chips):
         pl.semaphore_signal(
@@ -188,8 +174,7 @@
         )
     pl.semaphore_signal(barrier, inc=1, device_id=device(chip, 1 - core), device_id_type=MESH)
     mod_load.start()
-    for load in small_loads:
-        load.start()
+    join_load.start()
     step_value = jnp.full((1, TEMB), step_in[0].astype(jnp.float32))
     level_now = jnp.cos(0.5 * math.pi * step_value / STEPS)
     level_next = jnp.cos(0.5 * math.pi * (step_value + 1.0) / STEPS)
@@ -200,7 +185,7 @@
     angles = 1000.0 * level_now * frequency
     embedding = jnp.where(index < half_width, jnp.cos(angles), jnp.sin(angles))
     embedding = jnp.broadcast_to(embedding, (16, TEMB)).astype(jnp.bfloat16)
-    step_size = (level_next - level_now)[:, : latents.shape[1]]
+    step_size = level_next - level_now
     pl.semaphore_wait(barrier, chips)
 
     def piece_of(ref, target, piece):
@@ -252,11 +237,13 @@
     side.start()
 
     mod_load.wait()
-    block = 512
-    for start in range(0, w_mod.shape[1], block):
-        modulation[:, start : start + block] = jnp.dot(
-            embedding, w_mod[:, start : start + block], preferred_element_type=jnp.float32
+    for start in range(0, w_mod.shape[1], TEMB):
+        modulation[0:1, start : start + TEMB] = jnp.dot(
+            embedding, w_mod[:, start : start + TEMB], preferred_element_type=jnp.float32
         )[0:1]
+        modulation[1:2, start : start + TEMB] = step_size
+    terms_store = pltpu.make_async_copy(modulation, terms_ref, load_sem.at[2])
+    terms_store.start()
 
     lane = lax.broadcasted_iota(jnp.int32, (chips * tokens, LANES), 1)
 
@@ -361,7 +348,7 @@
             if distance < lines:
                 relay(distance, earlier)
 
-    small_loads[3].wait()
+    join_load.wait()
     side.wait_recv()
 
     def project(block_chip):
@@ -420,9 +407,8 @@
 
     for step in far_first:
         back(lax.rem(chip + step, chips), step).start()
-    update_in[chip] = update_out[chip]
-    for load in small_loads[:3]:
-        load.wait()
+    own_back = pltpu.make_async_copy(update_out.at[chip], update_in.at[chip], load_sem.at[3])
+    own_back.start()
     for step in range(1, chips):
         source = lax.rem(chip - step + chips, chips)
         remote(
@@ -432,26 +418,6 @@
             back_recv.at[source],
             device(source, core),
         ).wait_recv()
-    for source in range(chips):
-        cut = slice(source * width, (source + 1) * width)
-        summed[:, cut] = hidden[:, cut].astype(jnp.float32) + update_in[source].astype(jnp.float32)
-    whole = summed[...]
-    next_ref[...] = whole.astype(jnp.bfloat16)
-    average = jnp.mean(whole, axis=1, keepdims=True)
-    centered = whole - average
-    variance = jnp.mean(centered * centered, axis=1, keepdims=True)
-    shift_term = modulation[:, :D]
-    gain_term = modulation[:, D:]
-    normed = centered / jnp.sqrt(variance + 1e-05) * (1.0 + gain_term) + shift_term
-    velocity = lax.dot_general(
-        normed.astype(jnp.bfloat16),
-        w_out[...],
-        (((1,), (1,)), ((), ())),
-        preferred_element_type=jnp.float32,
-    )
-    velocity_ref[...] = velocity
-    latents_ref[...] = latents[...] + step_size * velocity
-
     for piece in range(pieces):
         for step in range(1, chips):
             swap(base_in, lax.rem(chip + step, chips), step, piece).wait_send()
@@ -465,61 +431,148 @@
                     distance, lambda o, p=piece: hand_on(o, p, lambda copy: copy.wait_send())
                 )
     side.wait_send()
+    terms_store.wait()
+    own_back.wait()
     for step in range(1, chips):
         back(lax.rem(chip + step, chips), step).wait_send()
+
+
+def finish_kernel(
+    update_in,
+    terms_in,
+    hidden_in,
+    latents_in,
+    out_in,
+    next_ref,
+    velocity_ref,
+    latents_ref,
+    update,
+    terms,
+    hidden,
+    latents,
+    w_out,
+    hidden_next,
+    velocity_out,
+    latents_next,
+    load_sem,
+    store_sem,
+):
+    loads = [
+        pltpu.make_async_copy(source, target, load_sem.at[number])
+        for number, (source, target) in enumerate(
+            (
+                (update_in, update),
+                (hidden_in, hidden),
+                (terms_in, terms),
+                (out_in, w_out),
+                (latents_in, latents),
+            )
+        )
+    ]
+    stores = [
+        pltpu.make_async_copy(source, target, store_sem.at[number])
+        for number, (source, target) in enumerate(
+            (
+                (hidden_next, next_ref),
+                (velocity_out, velocity_ref),
+                (latents_next, latents_ref),
+            )
+        )
+    ]
+    for load in loads:
+        load.start()
+    loads[0].wait()
+    loads[1].wait()
+    joined_columns = jnp.concatenate([update[p] for p in range(update.shape[0])], axis=1)
+    summed = hidden[...].astype(jnp.float32) + joined_columns.astype(jnp.float32)
+    hidden_next[...] = summed.astype(jnp.bfloat16)
+    stores[0].start()
+    average = jnp.mean(summed, axis=1, keepdims=True)
+    centered = summed - average
+    variance = jnp.mean(centered * centered, axis=1, keepdims=True)
+    loads[2].wait()
+    width = hidden.shape[1]
+    shift_term = terms[0:1, :width]
+    gain_term = terms[0:1, width:]
+    normed = centered / jnp.sqrt(variance + 1e-05) * (1.0 + gain_term) + shift_term
+    loads[3].wait()
+    velocity = lax.dot_general(
+        normed.astype(jnp.bfloat16),
+        w_out[...],
+        (((1,), (1,)), ((), ())),
+        preferred_element_type=jnp.float32,
+    )
+    velocity_out[...] = velocity
+    stores[1].start()
+    loads[4].wait()
+    latents_next[...] = latents[...] + terms[1:2, : latents.shape[1]] * velocity
+    stores[2].start()
+    for store in stores:
+        store.wait()
 
 
 def fused(plan, hidden, latents, base_qkv, control_qkv, step_index, w_join, w_mod, w_out):
     chips, rows, lines, width, pieces = plan
     tokens = hidden.shape[0]
     hbm_spec = pl.BlockSpec(memory_space=pltpu.HBM)
-    vmem_spec = pl.BlockSpec(memory_space=pltpu.VMEM)
     dma = pltpu.SemaphoreType.DMA
+    vmem_limit = 60 * 1024 * 1024
+    per_piece = [dma((chips, pieces))] * 4
+    update, terms = pl.pallas_call(
+        functools.partial(fused_kernel, plan),
+        out_shape=(
+            jax.ShapeDtypeStruct((chips, tokens, width), jnp.bfloat16),
+            jax.ShapeDtypeStruct((2, w_mod.shape[1]), jnp.float32),
+        ),
+        in_specs=[hbm_spec] * 2 + [pl.BlockSpec(memory_space=pltpu.SMEM)] + [hbm_spec] * 2,
+        out_specs=(hbm_spec,) * 2,
+        scratch_shapes=[
+            pltpu.VMEM(w_mod.shape, jnp.bfloat16),
+            pltpu.VMEM((2 * w_join.shape[1], w_join.shape[0]), jnp.bfloat16),
+            pltpu.VMEM((2, w_mod.shape[1]), jnp.float32),
+            pltpu.VMEM((chips, pieces, 3, tokens, LANES), jnp.bfloat16),
+            pltpu.VMEM((chips, pieces, 2, tokens, LANES), jnp.bfloat16),
+            pltpu.VMEM((chips, pieces, chips * tokens, LANES), jnp.bfloat16),
+            pltpu.VMEM((chips * tokens, width), jnp.float32),
+            pltpu.VMEM((chips, tokens, width), jnp.bfloat16),
+            dma((4,)),
+            dma((pieces,)),
+            *per_piece,
+            dma,
+            dma,
+            *per_piece,
+            dma((chips,)),
+            dma((chips,)),
+        ],
+        compiler_params=pltpu.CompilerParams(
+            collective_id=0, has_side_effects=True, vmem_limit_bytes=vmem_limit
+        ),
+        name="fused",
+    )(base_qkv, control_qkv, step_index, w_join.T, w_mod)
     return pl.pallas_call(
-        functools.partial(fused_kernel, plan),
+        finish_kernel,
         out_shape=(
             jax.ShapeDtypeStruct(hidden.shape, jnp.bfloat16),
             jax.ShapeDtypeStruct(latents.shape, jnp.float32),
             jax.ShapeDtypeStruct(latents.shape, jnp.float32),
         ),
-        in_specs=[hbm_spec] * 4
-        + [pl.BlockSpec(memory_space=pltpu.SMEM)]
-        + [hbm_spec] * 3,
-        out_specs=(vmem_spec,) * 3,
+        in_specs=[hbm_spec] * 5,
+        out_specs=(hbm_spec,) * 3,
         scratch_shapes=[
+            pltpu.VMEM(update.shape, jnp.bfloat16),
+            pltpu.VMEM(terms.shape, jnp.float32),
             pltpu.VMEM(hidden.shape, jnp.bfloat16),
             pltpu.VMEM(latents.shape, jnp.float32),
             pltpu.VMEM(w_out.shape[::-1], jnp.bfloat16),
-            pltpu.VMEM(w_mod.shape, jnp.bfloat16),
-            pltpu.VMEM((2 * w_join.shape[1], w_join.shape[0]), jnp.bfloat16),
-            pltpu.VMEM((1, w_mod.shape[1]), jnp.float32),
-            pltpu.VMEM((chips, pieces, 3, tokens, LANES), jnp.bfloat16),
-            pltpu.VMEM((chips, pieces, 2, tokens, LANES), jnp.bfloat16),
-            pltpu.VMEM((chips, pieces, chips * tokens, LANES), jnp.bfloat16),
-            pltpu.VMEM((chips * tokens, width), jnp.float32),
-            pltpu.VMEM((chips, tokens, width), jnp.bfloat16),
-            pltpu.VMEM((chips, tokens, width), jnp.bfloat16),
-            pltpu.VMEM(hidden.shape, jnp.float32),
+            pltpu.VMEM(hidden.shape, jnp.bfloat16),
+            pltpu.VMEM(latents.shape, jnp.float32),
+            pltpu.VMEM(latents.shape, jnp.float32),
             dma((5,)),
-            dma((pieces,)),
-            dma((chips, pieces)),
-            dma((chips, pieces)),
-            dma((chips, pieces)),
-            dma((chips, pieces)),
-            dma,
-            dma,
-            dma((chips, pieces)),
-            dma((chips, pieces)),
-            dma((chips, pieces)),
-            dma((chips, pieces)),
-            dma((chips,)),
-            dma((chips,)),
+            dma((3,)),
         ],
-        compiler_params=pltpu.CompilerParams(
-            collective_id=0, has_side_effects=True, vmem_limit_bytes=60 * 1024 * 1024
-        ),
-        name="fused",
-    )(hidden, latents, base_qkv, control_qkv, step_index, w_join.T, w_mod, w_out.T)
+        compiler_params=pltpu.CompilerParams(vmem_limit_bytes=vmem_limit),
+        name="norm_and_step",
+    )(update, terms, hidden, latents, w_out.T)
 
 
 def plan_for(count, sections_width, section_width):

time: 47 us -> 43.8 us (0.932)
  local copies, waits for them, and re-layouts: 4.19 us -> 0 us
  Pallas kernels: 41.2 us -> 42.4 us
    unnamed x3 -> x0, local copies, waits for them, and re-layouts: 4.19 us -> none
    pallas_call x0 -> x1, Pallas kernels: none -> 2.2 us  [fused(): pl.pallas_call(finish_kernel, out_shape=(jax.ShapeDtypeStruct(hidden.shap...]
    pallas_call x1, Pallas kernels: 41.2 us -> 40.2 us  [fused(): pl.pallas_call(functools.partial(fused_kernel, plan), out_shape=(jax.Shap...]
where the time goes in v4:
time: 43.8 us; the launch traced here: 43.7 us
  Pallas kernels  42.4 us (97%)
  between operations  1.29 us (3%)
    pallas_call x1, Pallas kernels, fused(): pl.pallas_call(functools.partial(fused_kernel, plan), out_shape=(jax.Shap...  40.2 us
    pallas_call x1, Pallas kernels, fused(): pl.pallas_call(finish_kernel, out_shape=(jax.ShapeDtypeStruct(hidden.shap...  2.2 us

profile of v4, /device:TPU:0, one launch (start us, length us, event | category | flops | bytes accessed | tf_op | source)
XLA Modules:
  0.0 43.7 jit_solution(16265968813496357967)
XLA Ops:
  1.3 40.2 %fused.1 = (bf16[8,24,384]{2,1,0:T(8,128)(2,1)}, f32[2,6144]{1,0:T(2,128)}) custom-call(bf16[3,24,1536]{2,1,0:T(8,128)(2,1)} %base_in.1, bf16[3,24,1536]{2,1,0:T(8,128)(2,1)} %control_in.1, s32[1]{0:T(128)S(6)} %copy.11.step_in, bf16[192,3072]{1,0:T(8,128)(2,1)} %bitcast.2, bf16[512,6144]{1,0:T(8,128)(2,1)} %mod_in.1), custom_call_target="tpu_custom_call" | custom-call | tf_op jit(solution)/shard_map/fused/pallas_call | solution.py:521
  41.5 2.2 %norm_and_step.1 = (bf16[24,3072]{1,0:T(8,128)(2,1)}, f32[24,64]{1,0:T(8,128)}, f32[24,64]{1,0:T(8,128)}) custom-call(bf16[8,24,384]{2,1,0:T(8,128)(2,1)} %get-tuple-element.5.update_in, f32[2,6144]{1,0:T(2,128)} %get-tuple-element.6.terms_in, bf16[24,3072]{1,0:T(8,128)(2,1)} %hidden_in.1, f32[24,64]{1,0:T(8,128)} %latents_in.1, bf16[64,3072]{1,0:T(8,128)(2,1)} %bitcast.3), custom_call_target="tpu_custom_call" | custom-call | tf_op jit(solution)/shard_map/norm_and_step/pallas_call | solution.py:552

commit v5 on v4

--- a/solution.py
+++ b/solution.py
@@ -288,6 +288,8 @@
 
     def hand_on(origin, piece, act):
         block_chip = origin * rows + row
+        for step in range(1, rows):
+            act(hop(block_chip, piece, cross_send, place * rows + other_row_step(step)))
 
         @pl.when((origin <= place) & (place < lines - 1))
         def _():
@@ -296,9 +298,6 @@
         @pl.when((origin >= place) & (place > 0))
         def _():
             act(hop(block_chip, piece, left_send, chip - rows))
-
-        for step in range(1, rows):
-            act(hop(block_chip, piece, cross_send, place * rows + other_row_step(step)))
 
     def at_distance(distance, act):
         @pl.when(place >= distance)
@@ -361,38 +360,28 @@
         )
 
     total[...] = jnp.zeros_like(total)
-    project(chip)
     done = {p: pieces - 1 - p for p in range(pieces)}
-    for distance in range(1, lines):
+    for distance in range(lines):
         for piece in range(pieces):
             if done[piece] < distance:
                 relay(distance, piece)
-                done[piece] = distance
-        at_distance(distance, lambda origin: project(origin * rows + row))
+        if distance == 0:
+            project(chip)
+        else:
+            at_distance(distance, lambda origin: project(origin * rows + row))
+
+    def cross(origin, step):
+        block_chip = origin * rows + other_row_step(step)
+        for piece in range(pieces):
+            arrive(block_chip, piece)
+        project(block_chip)
+
+    for distance in range(lines):
         for step in range(1, rows):
-
-            def cross(origin, s=step):
-                block_chip = origin * rows + other_row_step(s)
-                for piece in range(pieces):
-                    arrive(block_chip, piece)
-                project(block_chip)
-
-            if distance == 1:
-                cross(place)
-            if distance > 1:
-                at_distance(distance - 1, cross)
-    for step in range(1, rows):
-
-        def last_cross(origin, s=step):
-            block_chip = origin * rows + other_row_step(s)
-            for piece in range(pieces):
-                arrive(block_chip, piece)
-            project(block_chip)
-
-        if lines == 1:
-            last_cross(place)
-        else:
-            at_distance(lines - 1, last_cross)
+            if distance == 0:
+                cross(place, step)
+            else:
+                at_distance(distance, lambda origin, s=step: cross(origin, s))
 
     update_out[...] = total[...].reshape(chips, tokens, width).astype(jnp.bfloat16)
 

time: 43.8 us -> 43.8 us (level)
  no operation moved by 1% of the time
where the time goes in v5:
time: 43.8 us; the launch traced here: 43.7 us
  Pallas kernels  42.4 us (97%)
  between operations  1.29 us (3%)
    pallas_call x1, Pallas kernels, fused(): pl.pallas_call(functools.partial(fused_kernel, plan), out_shape=(jax.Shap...  40.2 us
    pallas_call x1, Pallas kernels, fused(): pl.pallas_call(finish_kernel, out_shape=(jax.ShapeDtypeStruct(hidden.shap...  2.2 us

profile of v5, /device:TPU:0, one launch (start us, length us, event | category | flops | bytes accessed | tf_op | source)
XLA Modules:
  0.0 43.7 jit_solution(14726947379963023272)
XLA Ops:
  1.3 40.2 %fused.1 = (bf16[8,24,384]{2,1,0:T(8,128)(2,1)}, f32[2,6144]{1,0:T(2,128)}) custom-call(bf16[3,24,1536]{2,1,0:T(8,128)(2,1)} %base_in.1, bf16[3,24,1536]{2,1,0:T(8,128)(2,1)} %control_in.1, s32[1]{0:T(128)S(6)} %copy.11.step_in, bf16[192,3072]{1,0:T(8,128)(2,1)} %bitcast.2, bf16[512,6144]{1,0:T(8,128)(2,1)} %mod_in.1), custom_call_target="tpu_custom_call" | custom-call | tf_op jit(solution)/shard_map/fused/pallas_call | solution.py:510
  41.5 2.2 %norm_and_step.1 = (bf16[24,3072]{1,0:T(8,128)(2,1)}, f32[24,64]{1,0:T(8,128)}, f32[24,64]{1,0:T(8,128)}) custom-call(bf16[8,24,384]{2,1,0:T(8,128)(2,1)} %get-tuple-element.5.update_in, f32[2,6144]{1,0:T(2,128)} %get-tuple-element.6.terms_in, bf16[24,3072]{1,0:T(8,128)(2,1)} %hidden_in.1, f32[24,64]{1,0:T(8,128)} %latents_in.1, bf16[64,3072]{1,0:T(8,128)(2,1)} %bitcast.3), custom_call_target="tpu_custom_call" | custom-call | tf_op jit(solution)/shard_map/norm_and_step/pallas_call | solution.py:541

commit v6 on v5

--- a/solution.py
+++ b/solution.py
@@ -227,12 +227,13 @@
         )
 
     side = remote(join_in, join_half(core), side_send, side_recv, device(chip, 1 - core))
+    def send_piece(step, piece):
+        target = lax.rem(chip + step, chips)
+        from_section(target, lambda ref: swap(ref, target, step, piece).start())
+
+    for step in far_first:
+        send_piece(step, 0)
     for piece in range(pieces):
-        for step in far_first:
-            target = lax.rem(chip + step, chips)
-            from_section(
-                target, lambda ref, t=target, s=step, p=piece: swap(ref, t, s, p).start()
-            )
         from_section(chip, lambda ref, p=piece: own_copy(ref, p).start())
     side.start()
 
@@ -328,7 +329,7 @@
     for piece in range(pieces):
         from_section(chip, lambda ref, p=piece: own_copy(ref, p).wait())
         pass_on(chip, piece).start()
-        for step in reversed(far_first):
+        for sent, step in enumerate(reversed(far_first)):
             source = lax.rem(chip - step + chips, chips)
             remote(
                 heads_own.at[source, piece],
@@ -338,6 +339,8 @@
                 device(source, core),
             ).wait_recv()
             pass_on(source, piece).start()
+            if piece + 1 < pieces:
+                send_piece(far_first[sent], piece + 1)
         for step in range(chips):
             pass_on(lax.rem(chip - step + chips, chips), piece).wait_recv()
         attention(piece)

time: 43.8 us -> 46.6 us (1.064)
  Pallas kernels: 42.4 us -> 45.2 us
    pallas_call x1, Pallas kernels: 40.2 us -> 43 us  [fused(): pl.pallas_call(functools.partial(fused_kernel, plan), out_shape=(jax.Shap...]
where the time goes in v6:
time: 46.6 us; the launch traced here: 46.4 us
  Pallas kernels  45.2 us (97%)
  between operations  1.29 us (3%)
    pallas_call x1, Pallas kernels, fused(): pl.pallas_call(functools.partial(fused_kernel, plan), out_shape=(jax.Shap...  43 us
    pallas_call x1, Pallas kernels, fused(): pl.pallas_call(finish_kernel, out_shape=(jax.ShapeDtypeStruct(hidden.shap...  2.2 us

profile of v6, /device:TPU:0, one launch (start us, length us, event | category | flops | bytes accessed | tf_op | source)
XLA Modules:
  0.0 46.4 jit_solution(11658990684764747806)
XLA Ops:
  1.3 43.0 %fused.1 = (bf16[8,24,384]{2,1,0:T(8,128)(2,1)}, f32[2,6144]{1,0:T(2,128)}) custom-call(bf16[3,24,1536]{2,1,0:T(8,128)(2,1)} %base_in.1, bf16[3,24,1536]{2,1,0:T(8,128)(2,1)} %control_in.1, s32[1]{0:T(128)S(6)} %copy.11.step_in, bf16[192,3072]{1,0:T(8,128)(2,1)} %bitcast.2, bf16[512,6144]{1,0:T(8,128)(2,1)} %mod_in.1), custom_call_target="tpu_custom_call" | custom-call | tf_op jit(solution)/shard_map/fused/pallas_call | solution.py:513
  44.2 2.2 %norm_and_step.1 = (bf16[24,3072]{1,0:T(8,128)(2,1)}, f32[24,64]{1,0:T(8,128)}, f32[24,64]{1,0:T(8,128)}) custom-call(bf16[8,24,384]{2,1,0:T(8,128)(2,1)} %get-tuple-element.5.update_in, f32[2,6144]{1,0:T(2,128)} %get-tuple-element.6.terms_in, bf16[24,3072]{1,0:T(8,128)(2,1)} %hidden_in.1, f32[24,64]{1,0:T(8,128)} %latents_in.1, bf16[64,3072]{1,0:T(8,128)(2,1)} %bitcast.3), custom_call_target="tpu_custom_call" | custom-call | tf_op jit(solution)/shard_map/norm_and_step/pallas_call | solution.py:544

commit v7 on v5

--- a/solution.py
+++ b/solution.py
@@ -129,6 +129,8 @@
     side_recv,
     right_send,
     left_send,
+    far_right_send,
+    far_left_send,
     cross_send,
     join_recv,
     back_send,
@@ -236,14 +238,15 @@
         from_section(chip, lambda ref, p=piece: own_copy(ref, p).start())
     side.start()
 
-    mod_load.wait()
-    for start in range(0, w_mod.shape[1], TEMB):
-        modulation[0:1, start : start + TEMB] = jnp.dot(
-            embedding, w_mod[:, start : start + TEMB], preferred_element_type=jnp.float32
-        )[0:1]
-        modulation[1:2, start : start + TEMB] = step_size
-    terms_store = pltpu.make_async_copy(modulation, terms_ref, load_sem.at[2])
-    terms_store.start()
+    mod_blocks = w_mod.shape[1] // TEMB
+
+    def modulate(first, last):
+        for block in range(first, last):
+            cut = slice(block * TEMB, (block + 1) * TEMB)
+            modulation[0:1, cut] = jnp.dot(
+                embedding, w_mod[:, cut], preferred_element_type=jnp.float32
+            )[0:1]
+            modulation[1:2, cut] = step_size
 
     lane = lax.broadcasted_iota(jnp.int32, (chips * tokens, LANES), 1)
 
@@ -286,18 +289,42 @@
     def other_row_step(step):
         return lax.rem(row + step, rows)
 
+    def to_other_rows(origin, piece, act):
+        for step in range(1, rows):
+            target = place * rows + other_row_step(step)
+            act(hop(origin * rows + row, piece, cross_send, target))
+
+    def hand_out(piece, act):
+        to_other_rows(place, piece, act)
+
+        @pl.when(place < lines - 2)
+        def _():
+            act(hop(chip, piece, far_right_send, chip + 2 * rows))
+
+        @pl.when(place > 1)
+        def _():
+            act(hop(chip, piece, far_left_send, chip - 2 * rows))
+
+        @pl.when(place < lines - 1)
+        def _():
+            act(hop(chip, piece, right_send, chip + rows))
+
+        @pl.when(place > 0)
+        def _():
+            act(hop(chip, piece, left_send, chip - rows))
+
     def hand_on(origin, piece, act):
         block_chip = origin * rows + row
-        for step in range(1, rows):
-            act(hop(block_chip, piece, cross_send, place * rows + other_row_step(step)))
-
-        @pl.when((origin <= place) & (place < lines - 1))
+
+        @pl.when((origin <= place - 2) & (place < lines - 1))
         def _():
             act(hop(block_chip, piece, right_send, chip + rows))
 
-        @pl.when((origin >= place) & (place > 0))
+        @pl.when((origin >= place + 2) & (place > 0))
         def _():
             act(hop(block_chip, piece, left_send, chip - rows))
+
+        to_other_rows(origin, piece, act)
 
     def at_distance(distance, act):
         @pl.when(place >= distance)
@@ -341,11 +368,7 @@
         for step in range(chips):
             pass_on(lax.rem(chip - step + chips, chips), piece).wait_recv()
         attention(piece)
-        hand_on(place, piece, lambda copy: copy.start())
-        for earlier in range(piece):
-            distance = piece - earlier
-            if distance < lines:
-                relay(distance, earlier)
+        hand_out(piece, lambda copy: copy.start())
 
     join_load.wait()
     side.wait_recv()
@@ -360,15 +383,17 @@
         )
 
     total[...] = jnp.zeros_like(total)
-    done = {p: pieces - 1 - p for p in range(pieces)}
+    mod_load.wait()
     for distance in range(lines):
-        for piece in range(pieces):
-            if done[piece] < distance:
-                relay(distance, piece)
         if distance == 0:
             project(chip)
         else:
+            for piece in range(pieces):
+                relay(distance, piece)
             at_distance(distance, lambda origin: project(origin * rows + row))
+        modulate(distance * mod_blocks // lines, (distance + 1) * mod_blocks // lines)
+    terms_store = pltpu.make_async_copy(modulation, terms_ref, load_sem.at[2])
+    terms_store.start()
 
     def cross(origin, step):
         block_chip = origin * rows + other_row_step(step)
@@ -414,7 +439,7 @@
             pass_on(source, piece).wait_send()
         for distance in range(lines):
             if distance == 0:
-                hand_on(place, piece, lambda copy: copy.wait_send())
+                hand_out(piece, lambda copy: copy.wait_send())
             else:
                 at_distance(
                     distance, lambda o, p=piece: hand_on(o, p, lambda copy: copy.wait_send())
@@ -530,6 +555,7 @@
             dma,
             dma,
             *per_piece,
+            *per_piece[:2],
             dma((chips,)),
             dma((chips,)),
         ],

time: 43.8 us -> 46 us (1.050)
  Pallas kernels: 42.4 us -> 44.5 us
    pallas_call x1, Pallas kernels: 40.2 us -> 42.3 us  [fused(): pl.pallas_call(functools.partial(fused_kernel, plan), out_shape=(jax.Shap...]
where the time goes in v7:
time: 46 us; the launch traced here: 45.8 us
  Pallas kernels  44.5 us (97%)
  between operations  1.29 us (3%)
    pallas_call x1, Pallas kernels, fused(): pl.pallas_call(functools.partial(fused_kernel, plan), out_shape=(jax.Shap...  42.3 us
    pallas_call x1, Pallas kernels, fused(): pl.pallas_call(finish_kernel, out_shape=(jax.ShapeDtypeStruct(hidden.shap...  2.2 us

profile of v7, /device:TPU:0, one launch (start us, length us, event | category | flops | bytes accessed | tf_op | source)
XLA Modules:
  0.0 45.8 jit_solution(11573096264486590701)
XLA Ops:
  1.3 42.3 %fused.1 = (bf16[8,24,384]{2,1,0:T(8,128)(2,1)}, f32[2,6144]{1,0:T(2,128)}) custom-call(bf16[3,24,1536]{2,1,0:T(8,128)(2,1)} %base_in.1, bf16[3,24,1536]{2,1,0:T(8,128)(2,1)} %control_in.1, s32[1]{0:T(128)S(6)} %copy.11.step_in, bf16[192,3072]{1,0:T(8,128)(2,1)} %bitcast.2, bf16[512,6144]{1,0:T(8,128)(2,1)} %mod_in.1), custom_call_target="tpu_custom_call" | custom-call | tf_op jit(solution)/shard_map/fused/pallas_call | solution.py:535
  43.6 2.2 %norm_and_step.1 = (bf16[24,3072]{1,0:T(8,128)(2,1)}, f32[24,64]{1,0:T(8,128)}, f32[24,64]{1,0:T(8,128)}) custom-call(bf16[8,24,384]{2,1,0:T(8,128)(2,1)} %get-tuple-element.5.update_in, f32[2,6144]{1,0:T(2,128)} %get-tuple-element.6.terms_in, bf16[24,3072]{1,0:T(8,128)(2,1)} %hidden_in.1, f32[24,64]{1,0:T(8,128)} %latents_in.1, bf16[64,3072]{1,0:T(8,128)(2,1)} %bitcast.3), custom_call_target="tpu_custom_call" | custom-call | tf_op jit(solution)/shard_map/norm_and_step/pallas_call | solution.py:567

commit v8 on v5

--- a/solution.py
+++ b/solution.py
@@ -283,13 +283,34 @@
             device(target, core),
         )
 
-    def other_row_step(step):
-        return lax.rem(row + step, rows)
+    other_row = rows - 1 - row
+
+    def along_line(origin, target, piece):
+        near = (origin == target - 1) | (origin == target + 1)
+        origin_end = (origin == 0) | (origin == lines - 1)
+        target_end = (target == 0) | (target == lines - 1)
+        chosen = jnp.logical_not(target_end) & origin_end
+        if piece == 0:
+            chosen = chosen | target_end
+        return near & chosen
+
+    def share_other_row(piece, act):
+        block_chip = place * rows + other_row
+
+        @pl.when((place < lines - 1) & along_line(place, place + 1, piece))
+        def _():
+            act(hop(block_chip, piece, right_send, chip + rows))
+
+        @pl.when((place > 0) & along_line(place, place - 1, piece))
+        def _():
+            act(hop(block_chip, piece, left_send, chip - rows))
 
     def hand_on(origin, piece, act):
         block_chip = origin * rows + row
-        for step in range(1, rows):
-            act(hop(block_chip, piece, cross_send, place * rows + other_row_step(step)))
+
+        @pl.when(jnp.logical_not(along_line(origin, place, piece)))
+        def _():
+            act(hop(block_chip, piece, cross_send, place * rows + other_row))
 
         @pl.when((origin <= place) & (place < lines - 1))
         def _():
@@ -319,6 +340,10 @@
         ).wait_recv()
 
     def relay(distance, piece):
+        if distance == 1:
+            arrive(place * rows + other_row, piece)
+            share_other_row(piece, lambda copy: copy.start())
+
         def act(origin):
             arrive(origin * rows + row, piece)
             hand_on(origin, piece, lambda copy: copy.start())
@@ -370,18 +395,15 @@
         else:
             at_distance(distance, lambda origin: project(origin * rows + row))
 
-    def cross(origin, step):
-        block_chip = origin * rows + other_row_step(step)
+    def cross(origin):
+        block_chip = origin * rows + other_row
         for piece in range(pieces):
             arrive(block_chip, piece)
         project(block_chip)
 
-    for distance in range(lines):
-        for step in range(1, rows):
-            if distance == 0:
-                cross(place, step)
-            else:
-                at_distance(distance, lambda origin, s=step: cross(origin, s))
+    project(place * rows + other_row)
+    for distance in range(1, lines):
+        at_distance(distance, cross)
 
     update_out[...] = total[...].reshape(chips, tokens, width).astype(jnp.bfloat16)
 
@@ -414,6 +436,7 @@
             pass_on(source, piece).wait_send()
         for distance in range(lines):
             if distance == 0:
+                share_other_row(piece, lambda copy: copy.wait_send())
                 hand_on(place, piece, lambda copy: copy.wait_send())
             else:
                 at_distance(
@@ -565,7 +588,7 @@
 
 
 def plan_for(count, sections_width, section_width):
-    if count % 4 != 0:
+    if count % 4 != 0 or count < 8:
         return None
     chips = count // 2
     width = sections_width // chips

time: 43.8 us -> 45.6 us (1.041)
  Pallas kernels: 42.4 us -> 44.2 us
    pallas_call x1, Pallas kernels: 40.2 us -> 42 us  [fused(): pl.pallas_call(functools.partial(fused_kernel, plan), out_shape=(jax.Shap...]
where the time goes in v8:
time: 45.6 us; the launch traced here: 45.5 us
  Pallas kernels  44.2 us (97%)
  between operations  1.29 us (3%)
    pallas_call x1, Pallas kernels, fused(): pl.pallas_call(functools.partial(fused_kernel, plan), out_shape=(jax.Shap...  42 us
    pallas_call x1, Pallas kernels, fused(): pl.pallas_call(finish_kernel, out_shape=(jax.ShapeDtypeStruct(hidden.shap...  2.2 us

profile of v8, /device:TPU:0, one launch (start us, length us, event | category | flops | bytes accessed | tf_op | source)
XLA Modules:
  0.0 45.5 jit_solution(3151240280028385755)
XLA Ops:
  1.3 42.0 %fused.1 = (bf16[8,24,384]{2,1,0:T(8,128)(2,1)}, f32[2,6144]{1,0:T(2,128)}) custom-call(bf16[3,24,1536]{2,1,0:T(8,128)(2,1)} %base_in.1, bf16[3,24,1536]{2,1,0:T(8,128)(2,1)} %control_in.1, s32[1]{0:T(128)S(6)} %copy.11.step_in, bf16[192,3072]{1,0:T(8,128)(2,1)} %bitcast.2, bf16[512,6144]{1,0:T(8,128)(2,1)} %mod_in.1), custom_call_target="tpu_custom_call" | custom-call | tf_op jit(solution)/shard_map/fused/pallas_call | solution.py:533
  43.3 2.2 %norm_and_step.1 = (bf16[24,3072]{1,0:T(8,128)(2,1)}, f32[24,64]{1,0:T(8,128)}, f32[24,64]{1,0:T(8,128)}) custom-call(bf16[8,24,384]{2,1,0:T(8,128)(2,1)} %get-tuple-element.5.update_in, f32[2,6144]{1,0:T(2,128)} %get-tuple-element.6.terms_in, bf16[24,3072]{1,0:T(8,128)(2,1)} %hidden_in.1, f32[24,64]{1,0:T(8,128)} %latents_in.1, bf16[64,3072]{1,0:T(8,128)(2,1)} %bitcast.3), custom_call_target="tpu_custom_call" | custom-call | tf_op jit(solution)/shard_map/norm_and_step/pallas_call | solution.py:564

commit v9 on v7

--- a/solution.py
+++ b/solution.py
@@ -238,15 +238,14 @@
         from_section(chip, lambda ref, p=piece: own_copy(ref, p).start())
     side.start()
 
-    mod_blocks = w_mod.shape[1] // TEMB
-
-    def modulate(first, last):
-        for block in range(first, last):
-            cut = slice(block * TEMB, (block + 1) * TEMB)
-            modulation[0:1, cut] = jnp.dot(
-                embedding, w_mod[:, cut], preferred_element_type=jnp.float32
-            )[0:1]
-            modulation[1:2, cut] = step_size
+    mod_load.wait()
+    for start in range(0, w_mod.shape[1], TEMB):
+        modulation[0:1, start : start + TEMB] = jnp.dot(
+            embedding, w_mod[:, start : start + TEMB], preferred_element_type=jnp.float32
+        )[0:1]
+        modulation[1:2, start : start + TEMB] = step_size
+    terms_store = pltpu.make_async_copy(modulation, terms_ref, load_sem.at[2])
+    terms_store.start()
 
     lane = lax.broadcasted_iota(jnp.int32, (chips * tokens, LANES), 1)
 
@@ -383,7 +382,6 @@
         )
 
     total[...] = jnp.zeros_like(total)
-    mod_load.wait()
     for distance in range(lines):
         if distance == 0:
             project(chip)
@@ -391,9 +389,6 @@
             for piece in range(pieces):
                 relay(distance, piece)
             at_distance(distance, lambda origin: project(origin * rows + row))
-        modulate(distance * mod_blocks // lines, (distance + 1) * mod_blocks // lines)
-    terms_store = pltpu.make_async_copy(modulation, terms_ref, load_sem.at[2])
-    terms_store.start()
 
     def cross(origin, step):
         block_chip = origin * rows + other_row_step(step)

time: 46 us -> 45.7 us (level)
  no operation moved by 1% of the time
where the time goes in v9:
time: 45.7 us; the launch traced here: 45.5 us
  Pallas kernels  44.2 us (97%)
  between operations  1.29 us (3%)
    pallas_call x1, Pallas kernels, fused(): pl.pallas_call(functools.partial(fused_kernel, plan), out_shape=(jax.Shap...  42 us
    pallas_call x1, Pallas kernels, fused(): pl.pallas_call(finish_kernel, out_shape=(jax.ShapeDtypeStruct(hidden.shap...  2.2 us

profile of v9, /device:TPU:0, one launch (start us, length us, event | category | flops | bytes accessed | tf_op | source)
XLA Modules:
  0.0 45.5 jit_solution(342362410710940626)
XLA Ops:
  1.3 42.0 %fused.1 = (bf16[8,24,384]{2,1,0:T(8,128)(2,1)}, f32[2,6144]{1,0:T(2,128)}) custom-call(bf16[3,24,1536]{2,1,0:T(8,128)(2,1)} %base_in.1, bf16[3,24,1536]{2,1,0:T(8,128)(2,1)} %control_in.1, s32[1]{0:T(128)S(6)} %copy.11.step_in, bf16[192,3072]{1,0:T(8,128)(2,1)} %bitcast.2, bf16[512,6144]{1,0:T(8,128)(2,1)} %mod_in.1), custom_call_target="tpu_custom_call" | custom-call | tf_op jit(solution)/shard_map/fused/pallas_call | solution.py:530
  43.3 2.2 %norm_and_step.1 = (bf16[24,3072]{1,0:T(8,128)(2,1)}, f32[24,64]{1,0:T(8,128)}, f32[24,64]{1,0:T(8,128)}) custom-call(bf16[8,24,384]{2,1,0:T(8,128)(2,1)} %get-tuple-element.5.update_in, f32[2,6144]{1,0:T(2,128)} %get-tuple-element.6.terms_in, bf16[24,3072]{1,0:T(8,128)(2,1)} %hidden_in.1, f32[24,64]{1,0:T(8,128)} %latents_in.1, bf16[64,3072]{1,0:T(8,128)(2,1)} %bitcast.3), custom_call_target="tpu_custom_call" | custom-call | tf_op jit(solution)/shard_map/norm_and_step/pallas_call | solution.py:562

commit v10 on v6

--- a/solution.py
+++ b/solution.py
@@ -188,9 +188,9 @@
     step_size = level_next - level_now
     pl.semaphore_wait(barrier, chips)
 
-    def piece_of(ref, target, piece):
-        start = lax.rem(target, per_section) * width + piece * LANES
-        return ref.at[:, :, pl.ds(pl.multiple_of(start, LANES), LANES)]
+    def part_of(ref, target):
+        start = lax.rem(target, per_section) * width
+        return ref.at[:, :, pl.ds(pl.multiple_of(start, LANES), width)]
 
     def from_section(target, act):
         @pl.when(target < per_section)
@@ -203,38 +203,32 @@
 
     far_first = sorted(range(1, chips), key=lambda step: abs(2 * step - chips))
 
-    def swap(ref, target, step, piece):
+    def swap(ref, target, step):
         return remote(
-            piece_of(ref, target, piece),
-            heads_own.at[chip, piece],
-            swap_send.at[step, piece],
-            swap_recv.at[chip, piece],
+            part_of(ref, target),
+            heads_own.at[chip],
+            swap_send.at[step],
+            swap_recv.at[chip],
             device(target, core),
         )
 
-    def own_copy(ref, piece):
-        return pltpu.make_async_copy(
-            piece_of(ref, chip, piece), heads_own.at[chip, piece], own_sem.at[piece]
-        )
-
-    def pass_on(source, piece):
+    def own_copy(ref):
+        return pltpu.make_async_copy(part_of(ref, chip), heads_own.at[chip], own_sem)
+
+    def pass_on(source):
         return remote(
-            heads_own.at[source, piece, 1:3],
-            heads_other.at[source, piece],
-            pass_send.at[source, piece],
-            pass_recv.at[source, piece],
+            heads_own.at[source, 1:3],
+            heads_other.at[source],
+            pass_send.at[source],
+            pass_recv.at[source],
             device(chip, 1 - core),
         )
 
     side = remote(join_in, join_half(core), side_send, side_recv, device(chip, 1 - core))
-    def send_piece(step, piece):
+    for step in far_first:
         target = lax.rem(chip + step, chips)
-        from_section(target, lambda ref: swap(ref, target, step, piece).start())
-
-    for step in far_first:
-        send_piece(step, 0)
-    for piece in range(pieces):
-        from_section(chip, lambda ref, p=piece: own_copy(ref, p).start())
+        from_section(target, lambda ref, t=target, s=step: swap(ref, t, s).start())
+    from_section(chip, lambda ref: own_copy(ref).start())
     side.start()
 
     mod_load.wait()
@@ -250,7 +244,7 @@
 
     def attention(piece):
         def rows_of(ref, kind):
-            part = ref[:, piece, kind].astype(jnp.float32)
+            part = ref[:, kind, :, piece * LANES : (piece + 1) * LANES].astype(jnp.float32)
             return part.reshape(chips * tokens, LANES)
 
         queries = rows_of(heads_own, 0) * HD ** (-0.5)
@@ -326,23 +320,21 @@
 
         at_distance(distance, act)
 
+    from_section(chip, lambda ref: own_copy(ref).wait())
+    pass_on(chip).start()
+    for step in reversed(far_first):
+        source = lax.rem(chip - step + chips, chips)
+        remote(
+            heads_own.at[source],
+            heads_own.at[source],
+            swap_send.at[step],
+            swap_recv.at[source],
+            device(source, core),
+        ).wait_recv()
+        pass_on(source).start()
+    for step in range(chips):
+        pass_on(lax.rem(chip - step + chips, chips)).wait_recv()
     for piece in range(pieces):
-        from_section(chip, lambda ref, p=piece: own_copy(ref, p).wait())
-        pass_on(chip, piece).start()
-        for sent, step in enumerate(reversed(far_first)):
-            source = lax.rem(chip - step + chips, chips)
-            remote(
-                heads_own.at[source, piece],
-                heads_own.at[source, piece],
-                swap_send.at[step, piece],
-                swap_recv.at[source, piece],
-                device(source, core),
-            ).wait_recv()
-            pass_on(source, piece).start()
-            if piece + 1 < pieces:
-                send_piece(far_first[sent], piece + 1)
-        for step in range(chips):
-            pass_on(lax.rem(chip - step + chips, chips), piece).wait_recv()
         attention(piece)
         hand_on(place, piece, lambda copy: copy.start())
         for earlier in range(piece):
@@ -410,11 +402,11 @@
             back_recv.at[source],
             device(source, core),
         ).wait_recv()
+    for step in range(1, chips):
+        swap(base_in, lax.rem(chip + step, chips), step).wait_send()
+    for source in range(chips):
+        pass_on(source).wait_send()
     for piece in range(pieces):
-        for step in range(1, chips):
-            swap(base_in, lax.rem(chip + step, chips), step, piece).wait_send()
-        for source in range(chips):
-            pass_on(source, piece).wait_send()
         for distance in range(lines):
             if distance == 0:
                 hand_on(place, piece, lambda copy: copy.wait_send())
@@ -522,14 +514,14 @@
             pltpu.VMEM(w_mod.shape, jnp.bfloat16),
             pltpu.VMEM((2 * w_join.shape[1], w_join.shape[0]), jnp.bfloat16),
             pltpu.VMEM((2, w_mod.shape[1]), jnp.float32),
-            pltpu.VMEM((chips, pieces, 3, tokens, LANES), jnp.bfloat16),
-            pltpu.VMEM((chips, pieces, 2, tokens, LANES), jnp.bfloat16),
+            pltpu.VMEM((chips, 3, tokens, width), jnp.bfloat16),
+            pltpu.VMEM((chips, 2, tokens, width), jnp.bfloat16),
             pltpu.VMEM((chips, pieces, chips * tokens, LANES), jnp.bfloat16),
             pltpu.VMEM((chips * tokens, width), jnp.float32),
             pltpu.VMEM((chips, tokens, width), jnp.bfloat16),
             dma((4,)),
-            dma((pieces,)),
-            *per_piece,
+            dma,
+            *[dma((chips,))] * 4,
             dma,
             dma,
             *per_piece,

time: 46.6 us -> 45.2 us (0.970)
  Pallas kernels: 45.2 us -> 43.8 us
    pallas_call x1, Pallas kernels: 43 us -> 41.6 us  [fused(): pl.pallas_call(functools.partial(fused_kernel, plan), out_shape=(jax.Shap...]
where the time goes in v10:
time: 45.2 us; the launch traced here: 45.1 us
  Pallas kernels  43.8 us (97%)
  between operations  1.29 us (3%)
    pallas_call x1, Pallas kernels, fused(): pl.pallas_call(functools.partial(fused_kernel, plan), out_shape=(jax.Shap...  41.6 us
    pallas_call x1, Pallas kernels, fused(): pl.pallas_call(finish_kernel, out_shape=(jax.ShapeDtypeStruct(hidden.shap...  2.2 us

profile of v10, /device:TPU:0, one launch (start us, length us, event | category | flops | bytes accessed | tf_op | source)
XLA Modules:
  0.0 45.1 jit_solution(14582910106932185376)
XLA Ops:
  1.3 41.6 %fused.1 = (bf16[8,24,384]{2,1,0:T(8,128)(2,1)}, f32[2,6144]{1,0:T(2,128)}) custom-call(bf16[3,24,1536]{2,1,0:T(8,128)(2,1)} %base_in.1, bf16[3,24,1536]{2,1,0:T(8,128)(2,1)} %control_in.1, s32[1]{0:T(128)S(6)} %copy.11.step_in, bf16[192,3072]{1,0:T(8,128)(2,1)} %bitcast.2, bf16[512,6144]{1,0:T(8,128)(2,1)} %mod_in.1), custom_call_target="tpu_custom_call" | custom-call | tf_op jit(solution)/shard_map/fused/pallas_call | solution.py:505
  42.9 2.2 %norm_and_step.1 = (bf16[24,3072]{1,0:T(8,128)(2,1)}, f32[24,64]{1,0:T(8,128)}, f32[24,64]{1,0:T(8,128)}) custom-call(bf16[8,24,384]{2,1,0:T(8,128)(2,1)} %get-tuple-element.5.update_in, f32[2,6144]{1,0:T(2,128)} %get-tuple-element.6.terms_in, bf16[24,3072]{1,0:T(8,128)(2,1)} %hidden_in.1, f32[24,64]{1,0:T(8,128)} %latents_in.1, bf16[64,3072]{1,0:T(8,128)(2,1)} %bitcast.3), custom_call_target="tpu_custom_call" | custom-call | tf_op jit(solution)/shard_map/norm_and_step/pallas_call | solution.py:536

commit v11 on v5

--- a/solution.py
+++ b/solution.py
@@ -328,7 +328,7 @@
     for piece in range(pieces):
         from_section(chip, lambda ref, p=piece: own_copy(ref, p).wait())
         pass_on(chip, piece).start()
-        for step in reversed(far_first):
+        for step in far_first:
             source = lax.rem(chip - step + chips, chips)
             remote(
                 heads_own.at[source, piece],

time: 43.8 us -> 43.8 us (level)
  no operation moved by 1% of the time
where the time goes in v11:
time: 43.8 us; the launch traced here: 43.6 us
  Pallas kernels  42.3 us (97%)
  between operations  1.29 us (3%)
    pallas_call x1, Pallas kernels, fused(): pl.pallas_call(functools.partial(fused_kernel, plan), out_shape=(jax.Shap...  40.1 us
    pallas_call x1, Pallas kernels, fused(): pl.pallas_call(finish_kernel, out_shape=(jax.ShapeDtypeStruct(hidden.shap...  2.2 us

profile of v11, /device:TPU:0, one launch (start us, length us, event | category | flops | bytes accessed | tf_op | source)
XLA Modules:
  0.0 43.6 jit_solution(17845978963327364095)
XLA Ops:
  1.3 40.1 %fused.1 = (bf16[8,24,384]{2,1,0:T(8,128)(2,1)}, f32[2,6144]{1,0:T(2,128)}) custom-call(bf16[3,24,1536]{2,1,0:T(8,128)(2,1)} %base_in.1, bf16[3,24,1536]{2,1,0:T(8,128)(2,1)} %control_in.1, s32[1]{0:T(128)S(6)} %copy.11.step_in, bf16[192,3072]{1,0:T(8,128)(2,1)} %bitcast.2, bf16[512,6144]{1,0:T(8,128)(2,1)} %mod_in.1), custom_call_target="tpu_custom_call" | custom-call | tf_op jit(solution)/shard_map/fused/pallas_call | solution.py:510
  41.4 2.2 %norm_and_step.1 = (bf16[24,3072]{1,0:T(8,128)(2,1)}, f32[24,64]{1,0:T(8,128)}, f32[24,64]{1,0:T(8,128)}) custom-call(bf16[8,24,384]{2,1,0:T(8,128)(2,1)} %get-tuple-element.5.update_in, f32[2,6144]{1,0:T(2,128)} %get-tuple-element.6.terms_in, bf16[24,3072]{1,0:T(8,128)(2,1)} %hidden_in.1, f32[24,64]{1,0:T(8,128)} %latents_in.1, bf16[64,3072]{1,0:T(8,128)(2,1)} %bitcast.3), custom_call_target="tpu_custom_call" | custom-call | tf_op jit(solution)/shard_map/norm_and_step/pallas_call | solution.py:541
